TPU v7x, 256 devices: a whole 4x4x8 slice. The times are simulated.
256 devices in a mesh: grp: 8 (over z), dev: 32 (over x, y, core).
Axes of the slice: x: 4, y: 4, z: 8, core: 2. Of those that a mesh axis runs over, the one named last changes fastest.
Arguments:
- node_rows: bfloat16 [196608, 1024], P(('grp', 'dev')), may hold values from -6 to 6
- w_self: bfloat16 [1024, 1024], replicated, may hold values from -0.1875 to 0.1875
- w_neigh: bfloat16 [1024, 1024], replicated, may hold values from -0.1875 to 0.1875
- hub_ids: int32 [64], replicated, may hold values from 0 to 196607, as said below
- bnd_idx: int32 [256, 32], P(('grp', 'dev')), may hold values from 0 to 767, as said below
- send_pos: int32 [256, 32, 64], P(('grp', 'dev')), may hold values from 0 to 31
- edge_src: int32 [1572864], P(('grp', 'dev')), may hold values from 0 to 2879, as said below
- edge_dst: int32 [1572864], P(('grp', 'dev')), may hold values from 0 to 767, as said below
Outputs:
- updated: bfloat16 [196608, 1024], P(('grp', 'dev'))
Inputs may be any that keep to these rules, and one draw needn't show every extreme that they name: `hub_ids`: distinct global node ids; no device owns more than 2 hubs, and some own exactly 2. `bnd_idx`: the 32 entries of each device are distinct local rows. `edge_src`: an entry below 768 is a local row; 768 + j * 64 + s is halo slot s from peer j; 2816 + k is hub k. `edge_dst`: every local node is the destination of at least one edge of its device.
All inputs are finite; a program needn't handle non-finite values.
Results may differ from a plain program's by a relative error of at most 0.0026.
Values may be sent and summed in bfloat16 or wider, within the bound.
A program may use at most 128 MiB of HBM per device.

v0:
```python
import jax
import jax.numpy as jnp
from jax import lax
from jax.sharding import PartitionSpec as P

NPD = 768


def body(node_rows, w_self, w_neigh, hub_ids, bnd_idx, send_pos, edge_src, edge_dst):
    device = lax.axis_index(("grp", "dev"))
    owner = hub_ids // NPD
    local_row = hub_ids % NPD
    picked = node_rows[local_row]
    mine = owner == device
    lowest = jnp.asarray(-jnp.inf, jnp.bfloat16)
    masked = jnp.where(mine[:, None], picked, lowest)
    hub_rows = lax.pmax(masked, ("grp", "dev"))
    outgoing = node_rows[bnd_idx[0][send_pos[0]]]
    incoming = lax.all_to_all(outgoing, "dev", split_axis=0, concat_axis=0, tiled=True)
    halo_rows = incoming.reshape(-1, node_rows.shape[1])
    row_table = jnp.concatenate([node_rows, halo_rows, hub_rows], axis=0)
    table_rows = row_table.shape[0]
    counts = jnp.zeros((NPD, table_rows), jnp.float32).at[edge_dst, edge_src].add(1.0)
    degree = jnp.sum(counts, axis=1)
    summed = jnp.dot(counts.astype(jnp.bfloat16), row_table, preferred_element_type=jnp.float32)
    neighbour_mean = (summed / degree[:, None]).astype(jnp.bfloat16)
    mixed = jnp.dot(node_rows, w_self, preferred_element_type=jnp.float32)
    mixed = mixed + jnp.dot(neighbour_mean, w_neigh, preferred_element_type=jnp.float32)
    return jnp.maximum(mixed, 0.0).astype(jnp.bfloat16)


def solution(mesh):
    in_specs = (
        P(("grp", "dev"), None),
        P(),
        P(),
        P(),
        P(("grp", "dev"), None),
        P(("grp", "dev"), None, None),
        P(("grp", "dev")),
        P(("grp", "dev")),
    )
    out_specs = P(("grp", "dev"), None)
    return jax.shard_map(body, mesh=mesh, in_specs=in_specs, out_specs=out_specs, check_vma=False)
```

profile of v0, /device:TPU:1, one launch (start us, length us, event | category | flops | bytes accessed | tf_op | source)
XLA Modules:
  0.0 327.9 jit_solution(14389841588739232258)
XLA Ops:
  6.5 0.0 copy-start
  6.5 0.0 copy-start.1
  6.5 0.9 compare_select_fusion.3
  7.4 0.1 reshape.53
  7.5 0.0 copy-done.1
  7.5 12.6 %gather_fusion = s32[2048]{0:T(1024)S(1)} fusion(s32[32]{0:T(128)S(1)} %bitcast.14, s32[2048]{0:T(1024)S(1)} %broadcast_clamp_fusion.1), kind=kCustom, calls=%fused_computation | custom fusion | bytes 24576 | tf_op jit(solution)/shard_map/gather | solution.py:18
  20.1 0.1 gather.12
  20.2 0.1 reshape.61
  20.3 12.6 %gather_fusion.1 = bf16[2048,1024]{1,0:T(8,128)(2,1)} fusion(bf16[768,1024]{1,0:T(8,128)(2,1)} %param.8, s32[2048]{0:T(1024)S(1)} %broadcast_clamp_fusion), kind=kCustom, calls=%fused_computation.1 | custom fusion | bytes 8396800 | tf_op jit(solution)/shard_map/gather | solution.py:18
  32.9 0.0 copy-start.6
  32.9 0.0 copy-start.2
  32.9 0.0 copy-start.3
  32.9 0.0 copy-start.5
  32.9 0.0 copy-start.4
  32.9 8.8 %all-to-all-start = ((bf16[32,64,1024]{2,1,0:T(8,128)(2,1)}), bf16[32,64,1024]{2,1,0:T(8,128)(2,1)}, u32[]{:S(2)}, u32[]{:S(2)}) async-start(bf16[32,64,1024]{2,1,0:T(8,128)(2,1)} %bitcast.15), calls=%async_computation | async-start | bytes 8388608 | tf_op jit(solution)/shard_map/all_to_all | solution.py:19
  41.7 0.0 all-reduce.2.cloned.1.call-start
  41.8 0.0 copy-done.6
  41.8 2.4 gather_fusion.2
  44.2 0.7 broadcast_select_fusion
  45.0 0.0 all-reduce.2.cloned.1.call-update
  45.0 0.0 copy-done.2
  45.0 0.0 copy-done.3
  45.0 0.0 copy-done.5
  45.1 0.1 multiply_reduce_fusion
  45.2 0.0 copy-done.4
  45.2 0.2 and_reduce_fusion
  45.4 0.0 copy-done
  45.4 4.8 %fusion.21 = f32[768,1024]{1,0:T(8,128)} fusion(bf16[768,1024]{1,0:T(8,128)(2,1)} %param.8, bf16[1024,1024]{1,0:T(8,128)(2,1)S(1)} %copy-done), kind=kOutput, calls=%fused_computation.33 | convolution fusion | flops 1610612736 | bytes 6815744 | tf_op jit(solution)/shard_map/dot_general | solution.py:27
  50.2 36.5 %scatter_custom_fusion = f32[2211840]{0:T(1024)} fusion(s32[6144]{0:T(1024)S(1)} %broadcast_select_fusion.1, f32[6144]{0:T(1024)S(1)} %broadcast.51, f32[]{:T(128)} %constant.13.clone.1), kind=kCustom, calls=%fused_computation.11 | custom fusion | flops 6144 | bytes 8847364
  86.7 10.4 %reshape.49 = f32[2880,768]{1,0:T(8,128)} reshape(f32[2211840]{0:T(1024)} %scatter_custom_fusion) | data formatting | bytes 17694720 | tf_op jit(solution)/shard_map/scatter-add | solution.py:23
  97.0 4.1 %reduce_sum.9 = f32[768]{0:T(1024)S(1)} reduce(f32[2880,768]{1,0:T(8,128)} %reshape.49, f32[]{:T(128)} %constant.13.clone.1), dimensions={0}, to_apply=%region_2.3 | reduce | flops 2211072 | bytes 8850436 | tf_op jit(solution)/shard_map/reduce_sum | solution.py:24
  101.1 205.3 %all-reduce.2.cloned.1.call-done = bf16[64,1024]{1,0:T(8,128)(2,1)} async-done(((bf16[64,1024]{1,0:T(8,128)(2,1)}), bf16[64,1024]{1,0:T(8,128)(2,1)}) %all-reduce.2.cloned.1.call-update) | async-done | bytes 131088 | tf_op jit(solution)/shard_map/pmax | solution.py:17
  306.5 0.0 all-to-all-done
  306.5 14.6 %maximum_convert_fusion = bf16[768,1024]{1,0:T(8,128)(2,1)} fusion(f32[768,1024]{1,0:T(8,128)} %fusion.21, bf16[1024,1024]{1,0:T(8,128)(2,1)} %param.10, f32[768]{0:T(1024)S(1)} %reduce_sum.9, bf16[64,1024]{1,0:T(8,128)(2,1)} %all-reduce.2.cloned.1.call-done, bf16[2048,1024]{1,0:T(8,128)(2,1)} %bitcast.5, bf16[768,1024]{1,0:T(8,128)(2,1)} %param.8, ...), kind=kOutput, calls=%fused_computation.13 | convolution fusion | flops 6164299776 | bytes 21564416 | tf_op jit(solution)/shard_map/dot_general | solution.py:28
  (10 shorter events, 0.1 us)
Async XLA Ops:
  6.5 38.8 %copy-start = (bf16[1024,1024]{1,0:T(8,128)(2,1)S(1)}, bf16[1024,1024]{1,0:T(8,128)(2,1)}, u32[]{:S(2)}) copy-start(bf16[1024,1024]{1,0:T(8,128)(2,1)} %param.9) | copy-start | bytes 6291460
  6.5 1.0 copy-start.1
  32.9 8.9 %copy-start.6 = (s32[64]{0:T(128)S(1)}, s32[64]{0:T(128)}, u32[]{:S(2)}) copy-start(s32[64]{0:T(128)} %param.11) | copy-start | bytes 772
  32.9 12.1 %copy-start.2 = (s32[6144]{0:T(1024)S(1)}, s32[6144]{0:T(1024)}, u32[]{:S(2)}) copy-start(s32[6144]{0:T(1024)} %param.15) | copy-start | bytes 73732
  32.9 12.1 %copy-start.3 = (s32[6144]{0:T(1024)S(1)}, s32[6144]{0:T(1024)}, u32[]{:S(2)}) copy-start(s32[6144]{0:T(1024)} %param.14) | copy-start | bytes 73732
  32.9 12.2 %copy-start.5 = (s32[2]{0:T(128)S(1)}, s32[2]{0:T(128)}, u32[]{:S(2)}) copy-start(s32[2]{0:T(128)} %constant.50) | copy-start | bytes 28
  32.9 12.3 %copy-start.4 = (s32[2]{0:T(128)S(1)}, s32[2]{0:T(128)}, u32[]{:S(2)}) copy-start(s32[2]{0:T(128)} %constant.53) | copy-start | bytes 28
  32.9 273.6 %all-to-all-start = ((bf16[32,64,1024]{2,1,0:T(8,128)(2,1)}), bf16[32,64,1024]{2,1,0:T(8,128)(2,1)}, u32[]{:S(2)}, u32[]{:S(2)}) async-start(bf16[32,64,1024]{2,1,0:T(8,128)(2,1)} %bitcast.15), calls=%async_computation | async-start | bytes 8388608 | tf_op jit(solution)/shard_map/all_to_all | solution.py:19
  41.7 264.8 %all-reduce.2.cloned.1.call-start = ((), (), s32[]{:S(2)}) async-start(), calls=%async_computation.1 | async-start | bytes 262144 | tf_op jit(solution)/shard_map/pmax | solution.py:17
Sparse Core Ops, SparseCore 0:
  48.1 258.3 all-reduce.1
where the time goes:
time: 329 us; the launch traced here: 328 us
  waiting for transfers between devices  205 us (62%)
  other arithmetic  42.5 us (13%)
  local copies, waits for them, and re-layouts  38.2 us (12%)
  matrix products  19.4 us (6%)
  between operations  13.5 us (4%)
  starting transfers between devices  8.83 us (3%)
    pmax x1, waiting for transfers between devices, body(): hub_rows = lax.pmax(masked, ('grp', 'dev'))  205 us
    unnamed x4, other arithmetic  36.8 us
    gather x3, local copies, waits for them, and re-layouts, body(): outgoing = node_rows[bnd_idx[0][send_pos[0]]]  25.3 us
    dot_general x1, matrix products, body(): jnp.dot(neighbour_mean, w_neigh, preferred_element_type=jnp.float32)  14.6 us
    scatter-add x1, local copies, waits for them, and re-layouts, body(): jnp.zeros((NPD, table_rows), jnp.float32).at[edge_dst, edge_src].add(1.0)  10.4 us
    all_to_all x1, starting transfers between devices, body(): lax.all_to_all(outgoing, 'dev', split_axis=0, concat_axis=0, tiled=True)  8.79 us
  transfers between devices with their start and end apart: 2, of which 1 were waited for; matrix products, arithmetic and copies ran while one was open for 18% of the time, Pallas kernels for 0%

commit v1 on v0

v1 whole, which is shorter than its diff:
```python
import jax
import jax.numpy as jnp
from jax import lax
from jax.experimental import pallas as pl
from jax.experimental.pallas import tpu as pltpu
from jax.sharding import PartitionSpec as P

D = 1024
NPD = 768
HUBS = 64
BND = 32
SLOT = 64
E_DEV = 6144
ROWS = E_DEV // 128
N_DEV = 32
N_GRP = 8
HALO = N_DEV * SLOT
STEP_ROWS = 12
STEP = STEP_ROWS * 128
COL = 256
DIGIT = 4096
MESH = pl.DeviceIdType.MESH
ONE_HOT = jnp.bfloat16
NT = (((1,), (1,)), ((), ()))
TN = (((0,), (0,)), ((), ()))


def kernel(node_hbm, ws_hbm, wn_hbm, hub_ids, bnd_idx, send_pos, edge_src, edge_dst,
           out_hbm,
           node, ws, wn, bnd, hubs, hmask, h1_recv, h2_out, h2_recv, sp_send, sp_recv,
           col_of, weight_of, one_dst, one_src, raw, halo_cnt, own_cnt, degree, acc, summed, mean, out_buf,
           in_sem, out_sem, blk_send, blk_recv, sib_send, sib_recv, small_send, small_recv):
    grp = lax.axis_index("grp")
    me = lax.axis_index("dev")
    x, y, c = me // 8, (me // 2) % 4, me % 2

    def at(dx, dy):
        return (((x + dx + 4) % 4) * 4 + (y + dy + 4) % 4) * 2 + c

    xm, xp, ym, yp = at(-1, 0), at(1, 0), at(0, -1), at(0, 1)
    sib = me + 1 - 2 * c

    node_in = pltpu.make_async_copy(node_hbm, node, in_sem.at[0])
    ws_in = pltpu.make_async_copy(ws_hbm, ws, in_sem.at[1])
    wn_in = pltpu.make_async_copy(wn_hbm, wn, in_sem.at[2])
    node_in.start()
    ws_in.start()
    wn_in.start()

    barrier = pltpu.get_barrier_semaphore()

    @pl.loop(1, N_DEV)
    def _(o):
        pl.semaphore_signal(barrier, inc=1, device_id=(grp, (me + o) % N_DEV), device_id_type=MESH)

    @pl.loop(1, N_GRP)
    def _(o):
        pl.semaphore_signal(barrier, inc=1, device_id=((grp + o) % N_GRP, me), device_id_type=MESH)

    for j in range(N_DEV):
        sp_send[j, 0:1, 0:SLOT] = send_pos[0, j : j + 1, :]

    node_in.wait()
    row_id = lax.broadcasted_iota(jnp.int32, (NPD, BND), 0)
    pick = jnp.where(row_id == bnd_idx[...], 1.0, 0.0).astype(jnp.bfloat16)
    rows = lax.dot_general(pick, node[...], TN, preferred_element_type=jnp.float32)
    bnd[pl.ds(pl.multiple_of(me * BND, BND), BND), :] = rows.astype(jnp.bfloat16)
    local = hub_ids[...] - (grp * N_DEV + me) * NPD
    row_id = lax.broadcasted_iota(jnp.int32, (NPD, HUBS), 0)
    pick = jnp.where(row_id == local, 1.0, 0.0).astype(jnp.bfloat16)
    rows = lax.dot_general(pick, node[...], TN, preferred_element_type=jnp.float32)
    hmask[...] = rows.astype(jnp.bfloat16)

    pl.semaphore_wait(barrier, N_DEV - 1 + N_GRP - 1)

    def piece(dev, lo, n, left, width):
        return bnd.at[pl.ds(pl.multiple_of(dev * BND + lo, 16), n), pl.ds(left, width)]

    def push(dev, to, phase, lo=0, n=BND, left=0, width=D):
        ref = piece(dev, lo, n, left, width)
        pltpu.make_async_remote_copy(ref, ref, blk_send, blk_recv.at[phase], device_id=(grp, to), device_id_type=MESH).start()

    def to_sib(dev, phase):
        ref = piece(dev, 0, BND, 0, D)
        pltpu.make_async_remote_copy(ref, ref, sib_send, sib_recv.at[phase], device_id=(grp, sib), device_id_type=MESH).start()

    def wait_rows(sem, n):
        ref = bnd.at[pl.ds(0, n), :]
        pltpu.make_async_copy(ref, ref, sem).wait()

    hub_row, hub_col = pl.multiple_of(16 * (me // 8), 16), pl.multiple_of(128 * (me % 8), 128)

    for to in (xm, xp, ym, yp):
        push(me, to, 0)

    @pl.loop(1, N_DEV)
    def _(o):
        to = (me + o) % N_DEV
        pltpu.make_async_remote_copy(sp_send.at[to], sp_recv.at[o - 1], small_send.at[0], small_recv.at[0],
                                     device_id=(grp, to), device_id_type=MESH).start()

    @pl.loop(1, N_DEV)
    def _(o):
        to = (me + o) % N_DEV
        src = hmask.at[pl.ds(pl.multiple_of(16 * (to // 8), 16), 16), pl.ds(pl.multiple_of(128 * (to % 8), 128), 128)]
        pltpu.make_async_remote_copy(src, h1_recv.at[o - 1], small_send.at[1], small_recv.at[1],
                                     device_id=(grp, to), device_id_type=MESH).start()

    to_sib(me, 0)
    sp_recv[N_DEV - 1] = sp_send[me]

    ws_in.wait()

    @pl.loop(0, D // COL)
    def _(i):
        cols = pl.ds(pl.multiple_of(i * COL, COL), COL)
        acc[:, cols] = jnp.dot(node[...], ws[:, cols], preferred_element_type=jnp.float32)

    wait_rows(blk_recv.at[0], 4 * BND)
    push(xm, xp, 1, 0, BND, 0, D // 2)
    push(xp, xm, 1, 0, BND, D // 2, D // 2)
    push(ym, yp, 1, 0, BND, 0, D // 2)
    push(yp, ym, 1, 0, BND, D // 2, D // 2)
    for from_x in (xm, xp):
        for to in (ym, yp):
            push(from_x, to, 1, 0, 16)
    for from_y in (ym, yp):
        for to in (xm, xp):
            push(from_y, to, 1, 16, 16)
    for dev in (xm, xp, ym, yp):
        to_sib(dev, 1)

    pltpu.make_async_copy(sp_recv.at[pl.ds(0, N_DEV - 1)], sp_recv.at[pl.ds(0, N_DEV - 1)], small_recv.at[0]).wait()
    src = edge_src[...]
    slot = src - NPD
    is_halo = jnp.logical_and(slot >= 0, slot < HALO)
    peer = jnp.where(is_halo, slot // SLOT, -1)
    within = jnp.where(is_halo, slot % SLOT, 0)
    weight_of[...] = jnp.where(is_halo, 1.0, float(DIGIT))
    col_of[...] = jnp.where(src >= NPD + HALO, src - HALO, src)

    @pl.loop(0, N_DEV)
    def _(j):
        table = jnp.broadcast_to(sp_recv[(me - j - 1 + N_DEV) % N_DEV], (ROWS, 128))
        found = jnp.take_along_axis(table, within, axis=1)
        col_of[...] = jnp.where(peer == j, found + j * BND, col_of[...])

    def count_step(step):
        @pl.loop(0, STEP_ROWS)
        def _(r):
            row = step * STEP_ROWS + r
            here = pl.ds(pl.multiple_of(r * 128, 128), 128)
            d = edge_dst[pl.ds(row, 1), :].astype(jnp.int16)
            s = col_of[pl.ds(row, 1), :].astype(jnp.int16)
            w = weight_of[pl.ds(row, 1), :].astype(jnp.bfloat16)
            zero = jnp.zeros((), jnp.bfloat16)
            one = jnp.ones((), jnp.bfloat16)
            id_d = lax.broadcasted_iota(jnp.int16, (NPD, 128), 0)
            one_dst[:, here] = jnp.where(id_d == d, one, zero).astype(ONE_HOT)
            id_s = lax.broadcasted_iota(jnp.int16, (D, 128), 0)
            one_src[:, here] = jnp.where(id_s == s, jnp.broadcast_to(w, (D, 128)), zero).astype(ONE_HOT)

        @pl.loop(0, D // COL)
        def _(i):
            cols = pl.ds(pl.multiple_of(i * COL, COL), COL)
            part = lax.dot_general(one_dst[...], one_src[cols, :], NT, preferred_element_type=jnp.float32)
            if step % 2 == 0:
                raw[step // 2, :, cols] = part
            else:
                raw[step // 2, :, cols] += part

    count_step(0)

    pltpu.make_async_copy(h1_recv, h1_recv, small_recv.at[1]).wait()
    block = jnp.sum(h1_recv[...].astype(jnp.float32), axis=0)
    block = block + hmask[pl.ds(hub_row, 16), pl.ds(hub_col, 128)].astype(jnp.float32)
    h2_out[0] = block.astype(jnp.bfloat16)

    @pl.loop(1, N_GRP)
    def _(o):
        pltpu.make_async_remote_copy(h2_out.at[0], h2_recv.at[o - 1], small_send.at[2], small_recv.at[2],
                                     device_id=((grp + o) % N_GRP, me), device_id_type=MESH).start()

    x2, y2 = at(2, 0), at(0, 2)
    mm, mp, pm, pp = at(-1, -1), at(-1, 1), at(1, -1), at(1, 1)
    wait_rows(blk_recv.at[1], 12 * 16)
    for to in (ym, yp):
        push(x2, to, 2, 0, 16)
    for to in (xm, xp):
        push(y2, to, 2, 16, 16)
    for dev in (mm, pm):
        push(dev, yp, 2, 0, 16, 0, D // 2)
    for dev in (mp, pp):
        push(dev, ym, 2, 0, 16, D // 2, D // 2)
    for dev in (mm, mp):
        push(dev, xp, 2, 16, 16, 0, D // 2)
    for dev in (pm, pp):
        push(dev, xm, 2, 16, 16, D // 2, D // 2)
    for dev in (x2, y2, mm, mp, pm, pp):
        to_sib(dev, 2)

    count_step(1)

    pltpu.make_async_copy(h2_recv, h2_recv, small_recv.at[2]).wait()
    block = jnp.sum(h2_recv[...].astype(jnp.float32), axis=0) + h2_out[0].astype(jnp.float32)
    mine = hubs.at[pl.ds(hub_row, 16), pl.ds(hub_col, 128)]
    mine[...] = block.astype(jnp.bfloat16)

    @pl.loop(1, N_DEV)
    def _(o):
        pltpu.make_async_remote_copy(mine, mine, small_send.at[3], small_recv.at[3],
                                     device_id=(grp, (me + o) % N_DEV), device_id_type=MESH).start()

    wait_rows(blk_recv.at[2], 8 * 16)
    x2m, x2p, m2, p2 = at(2, -1), at(2, 1), at(-1, 2), at(1, 2)
    push(x2m, yp, 3, 0, 16, 0, D // 2)
    push(x2p, ym, 3, 0, 16, D // 2, D // 2)
    push(m2, xp, 3, 16, 16, 0, D // 2)
    push(p2, xm, 3, 16, 16, D // 2, D // 2)
    for dev in (x2m, x2p, m2, p2):
        to_sib(dev, 3)

    count_step(2)

    wait_rows(blk_recv.at[3], BND)
    to_sib(at(2, 2), 4)

    count_step(3)

    degree[...] = jnp.zeros_like(degree)

    @pl.loop(0, D // COL)
    def _(i):
        cols = pl.ds(pl.multiple_of(i * COL, COL), COL)
        first, second = raw[0, :, cols], raw[1, :, cols]
        high_a, high_b = jnp.floor(first * (1.0 / DIGIT)), jnp.floor(second * (1.0 / DIGIT))
        high = high_a + high_b
        low = (first - high_a * DIGIT) + (second - high_b * DIGIT)
        own_cnt[:, cols] = high.astype(jnp.bfloat16)
        halo_cnt[:, cols] = low.astype(jnp.bfloat16)
        degree[...] += jnp.sum(high + low, axis=1, keepdims=True)

    @pl.loop(0, D // COL)
    def _(i):
        cols = pl.ds(pl.multiple_of(i * COL, COL), COL)
        summed[:, cols] = jnp.dot(own_cnt[:, 0:NPD], node[:, cols], preferred_element_type=jnp.float32)

    wait_rows(sib_recv.at[0], BND)
    wait_rows(sib_recv.at[1], 4 * BND)
    wait_rows(sib_recv.at[2], 6 * BND)
    wait_rows(sib_recv.at[3], 4 * BND)
    wait_rows(sib_recv.at[4], BND)
    pltpu.make_async_copy(h1_recv, h1_recv, small_recv.at[3]).wait()
    inverse = 1.0 / degree[...]

    @pl.loop(0, D // COL)
    def _(i):
        cols = pl.ds(pl.multiple_of(i * COL, COL), COL)
        total = summed[:, cols] + jnp.dot(halo_cnt[...], bnd[:, cols], preferred_element_type=jnp.float32)
        total = total + jnp.dot(own_cnt[:, NPD : NPD + HUBS], hubs[:, cols], preferred_element_type=jnp.float32)
        mean[:, cols] = (total * inverse).astype(jnp.bfloat16)

    wn_in.wait()

    @pl.loop(0, D // COL)
    def _(i):
        cols = pl.ds(pl.multiple_of(i * COL, COL), COL)
        mixed = acc[:, cols] + jnp.dot(mean[...], wn[:, cols], preferred_element_type=jnp.float32)
        out_buf[:, cols] = jnp.maximum(mixed, 0.0).astype(jnp.bfloat16)
        pltpu.make_async_copy(out_buf.at[:, cols], out_hbm.at[:, cols], out_sem).start()

    wait_rows(blk_send, 4 * BND + 12 * 16 + 8 * 16 + BND)
    wait_rows(sib_send, 16 * BND)
    pltpu.make_async_copy(sp_recv.at[pl.ds(0, N_DEV - 1)], sp_recv.at[pl.ds(0, N_DEV - 1)], small_send.at[0]).wait()
    pltpu.make_async_copy(h1_recv, h1_recv, small_send.at[1]).wait()
    pltpu.make_async_copy(h2_recv, h2_recv, small_send.at[2]).wait()
    pltpu.make_async_copy(h1_recv, h1_recv, small_send.at[3]).wait()
    pltpu.make_async_copy(out_buf, out_hbm, out_sem).wait()


def body(node_rows, w_self, w_neigh, hub_ids, bnd_idx, send_pos, edge_src, edge_dst):
    bf16, f32, i32 = jnp.bfloat16, jnp.float32, jnp.int32
    any_, vmem = pl.BlockSpec(memory_space=pl.ANY), pl.BlockSpec(memory_space=pltpu.VMEM)
    scratch = [
        pltpu.VMEM((NPD, D), bf16),
        pltpu.VMEM((D, D), bf16),
        pltpu.VMEM((D, D), bf16),
        pltpu.VMEM((N_DEV * BND, D), bf16),
        pltpu.VMEM((HUBS, D), bf16),
        pltpu.VMEM((HUBS, D), bf16),
        pltpu.VMEM((N_DEV - 1, 16, 128), bf16),
        pltpu.VMEM((1, 16, 128), bf16),
        pltpu.VMEM((N_GRP - 1, 16, 128), bf16),
        pltpu.VMEM((N_DEV, 1, 128), i32),
        pltpu.VMEM((N_DEV, 1, 128), i32),
        pltpu.VMEM((ROWS, 128), i32),
        pltpu.VMEM((ROWS, 128), f32),
        pltpu.VMEM((NPD, STEP), ONE_HOT),
        pltpu.VMEM((D, STEP), ONE_HOT),
        pltpu.VMEM((2, NPD, D), f32),
        pltpu.VMEM((NPD, D), bf16),
        pltpu.VMEM((NPD, D), bf16),
        pltpu.VMEM((NPD, 1), f32),
        pltpu.VMEM((NPD, D), f32),
        pltpu.VMEM((NPD, D), f32),
        pltpu.VMEM((NPD, D), bf16),
        pltpu.VMEM((NPD, D), bf16),
        pltpu.SemaphoreType.DMA((3,)),
        pltpu.SemaphoreType.DMA,
        pltpu.SemaphoreType.DMA,
        pltpu.SemaphoreType.DMA((4,)),
        pltpu.SemaphoreType.DMA,
        pltpu.SemaphoreType.DMA((5,)),
        pltpu.SemaphoreType.DMA((4,)),
        pltpu.SemaphoreType.DMA((4,)),
    ]
    return pl.pallas_call(
        kernel,
        out_shape=jax.ShapeDtypeStruct((NPD, D), bf16),
        in_specs=[any_, any_, any_, vmem, vmem, vmem, vmem, vmem],
        out_specs=any_,
        scratch_shapes=scratch,
        compiler_params=pltpu.CompilerParams(
            collective_id=0, has_side_effects=True, vmem_limit_bytes=56 * 2**20
        ),
        name="sage",
    )(
        node_rows, w_self, w_neigh, hub_ids.reshape(1, HUBS), bnd_idx, send_pos,
        edge_src.reshape(ROWS, 128), edge_dst.reshape(ROWS, 128),
    )


def solution(mesh):
    in_specs = (
        P(("grp", "dev"), None),
        P(),
        P(),
        P(),
        P(("grp", "dev"), None),
        P(("grp", "dev"), None, None),
        P(("grp", "dev")),
        P(("grp", "dev")),
    )
    out_specs = P(("grp", "dev"), None)
    return jax.shard_map(body, mesh=mesh, in_specs=in_specs, out_specs=out_specs, check_vma=False)
```

time: 329 us -> 50.2 us (0.15)
  waiting for transfers between devices: 205 us -> 0 us
  Pallas kernels: 0 us -> 47.4 us
  other arithmetic: 42.5 us -> 0 us
  local copies, waits for them, and re-layouts: 38.2 us -> 2.67 us
  matrix products: 19.4 us -> 0 us
  between operations: 13.5 us -> 0.01 us
  starting transfers between devices: 8.83 us -> 0 us
    pmax x1 -> x0, waiting for transfers between devices: 205 us -> none  [body(): hub_rows = lax.pmax(masked, ('grp', 'dev'))]
    pallas_call x0 -> x1, Pallas kernels: none -> 47.4 us  [body(): pl.pallas_call(kernel, out_shape=jax.ShapeDtypeStruct((NPD, D), bf16), in...]
    unnamed x4 -> x0, other arithmetic: 36.8 us -> none
    gather x4 -> x0, local copies, waits for them, and re-layouts: 27.7 us -> none  [the longest x3 25.3 us: body(): outgoing = node_rows[bnd_idx[0][send_pos[0]]]]
    dot_general x2 -> x0, matrix products: 19.4 us -> none  [the longest x1 14.6 us: body(): jnp.dot(neighbour_mean, w_neigh, preferred_element_type=jnp.float32)]
    scatter-add x1 -> x0, local copies, waits for them, and re-layouts: 10.4 us -> none  [body(): jnp.zeros((NPD, table_rows), jnp.float32).at[edge_dst, edge_src].add(1.0)]
    all_to_all x1 -> x0, starting transfers between devices: 8.79 us -> none  [body(): lax.all_to_all(outgoing, 'dev', split_axis=0, concat_axis=0, tiled=True)]
    reduce_sum x1 -> x0, other arithmetic: 4.07 us -> none  [body(): degree = jnp.sum(counts, axis=1)]
  transfers between devices with their start and end apart: 2 -> 0, of which waited for: 1 -> 0; matrix products, arithmetic and copies ran while one was open for 18% -> 0% of each run, Pallas kernels for 0% -> 0%
where the time goes in v1:
time: 50.2 us; the launch traced here: 50.1 us
  Pallas kernels  47.4 us (94%)
  local copies, waits for them, and re-layouts  2.67 us (5%)
    pallas_call x1, Pallas kernels, body(): pl.pallas_call(kernel, out_shape=jax.ShapeDtypeStruct((NPD, D), bf16), in...  47.4 us
    unnamed x1, local copies, waits for them, and re-layouts  2.67 us

profile of v1, /device:TPU:1, one launch (start us, length us, event | category | flops | bytes accessed | tf_op | source)
XLA Modules:
  0.0 50.1 jit_solution(2231416639822264659)
XLA Ops:
  0.0 47.4 %sage.1 = bf16[768,1024]{1,0:T(8,128)(2,1)} custom-call(bf16[768,1024]{1,0:T(8,128)(2,1)} %node_hbm.1, bf16[1024,1024]{1,0:T(8,128)(2,1)} %ws_hbm.1, bf16[1024,1024]{1,0:T(8,128)(2,1)} %wn_hbm.1, s32[1,64]{1,0:T(1,128)} %bitcast.5, s32[1,32]{1,0:T(1,128)} %bnd_idx.1, s32[1,32,64]{2,1,0:T(8,128)} %send_pos.1, s32[48,128]{1,0:T(8,128)} %bitcast.3, ...), custom_call_target="tpu_custom_call" | custom-call | tf_op jit(solution)/shard_map/sage/pallas_call | solution.py:317
  47.4 2.7 %copy.10 = bf16[768,1024]{1,0:T(8,128)(2,1)} copy(bf16[768,1024]{1,0:T(8,128)(2,1)} %sage.1) | data formatting | bytes 3145728

commit v2 on v0

v2 whole, which is shorter than its diff:
```python
import jax
import jax.numpy as jnp
from jax import lax
from jax.experimental import pallas as pl
from jax.experimental.pallas import tpu as pltpu
from jax.sharding import PartitionSpec as P

D = 1024
NPD = 768
HUBS = 64
BND = 32
SLOT = 64
E_DEV = 6144
ROWS = E_DEV // 128
N_DEV = 32
N_GRP = 8
HALO = N_DEV * SLOT
COLUMN = 2 * N_GRP
STEPS = 4
STEP_ROWS = ROWS // STEPS
STEP = STEP_ROWS * 128
HALO_DIGITS, HALO_BITS, HALO_LINES = 11, 2, 192
OWN_DIGITS, OWN_BITS, OWN_LINES, HUB_LINES = 8, 3, 96, 8
HUB_AT = HALO_LINES + OWN_LINES
DEGREE_AT = HUB_AT + HUB_LINES
LINES = DEGREE_AT + 8
LIMIT = 2.0**24
MESH = pl.DeviceIdType.MESH
NT = (((1,), (1,)), ((), ()))
TN = (((0,), (0,)), ((), ()))
BF16, F32, I32, I16 = jnp.bfloat16, jnp.float32, jnp.int32, jnp.int16


def dot(a, b, dims=(((1,), (0,)), ((), ()))):
    return lax.dot_general(a, b, dims, preferred_element_type=F32)


def place(dev, me):
    core = dev & 1
    dx = ((dev >> 3) - (me >> 3)) & 3
    dy = ((dev >> 1) - (me >> 1)) & 3
    du = jnp.where(core == 0, dx, dy)
    dv = jnp.where(core == 0, dy, dx)
    return 16 * (core ^ (me & 1)) + 4 * dv + du


def edge_column(src, me):
    slot = src - NPD
    is_halo = jnp.logical_and(slot >= 0, slot < HALO)
    halo = place((slot >> 6) & 31, me) * SLOT + (slot & 63)
    return jnp.where(is_halo, halo, jnp.where(src < NPD, src + HALO, src))


def hub_owner_rank(hub_ids):
    owner = hub_ids // NPD
    lines = lax.broadcasted_iota(I32, (N_DEV * N_GRP, HUBS), 0)
    member = jnp.where(lines == owner, 1.0, 0.0).astype(BF16)
    same = dot(member, member, TN)
    earlier = lax.broadcasted_iota(I32, (HUBS, HUBS), 0) < lax.broadcasted_iota(I32, (HUBS, HUBS), 1)
    rank = jnp.sum(jnp.where(earlier, same, 0.0), axis=0, keepdims=True)
    return owner, rank.astype(I32)


def main_kernel(node_hbm, ws_hbm, wn_hbm, hub_ids, bnd_idx, send_pos, edge_src, edge_dst,
                out_hbm, bnd_hbm, hubs_hbm, remap_hbm, flag,
                node, ws, wn, bnd, pos, column, hubs, tile_z, remap,
                line_of, weight_of, one_dst_a, one_dst_b, one_src_a, one_src_b, packed,
                halo_cnt, own_cnt, bnd_cnt, acc, summed, out_buf,
                in_sem, out_sem, b_send, b_sib_send, p_send, p_sib_send, h_send, h_sib_send, z_send, recv):
    grp = lax.axis_index("grp")
    me = lax.axis_index("dev")
    x, y, c = me // 8, (me // 2) % 4, me % 2
    sib = me + 1 - 2 * c

    def at(du, dv):
        dx, dy = du * (1 - c) + dv * c, dv * (1 - c) + du * c
        return (((x + dx) % 4) * 4 + (y + dy) % 4) * 2 + c

    node_in = pltpu.make_async_copy(node_hbm, node, in_sem.at[0])
    ws_in = pltpu.make_async_copy(ws_hbm, ws, in_sem.at[1])
    wn_in = pltpu.make_async_copy(wn_hbm, wn, in_sem.at[2])
    node_in.start()
    ws_in.start()
    wn_in.start()

    barrier = pltpu.get_barrier_semaphore()
    for near in [at(1, 0), at(3, 0), at(2, 0), at(0, 1), at(0, 3), at(0, 2), sib]:
        pl.semaphore_signal(barrier, inc=1, device_id=(grp, near), device_id_type=MESH)
    for o in range(1, N_GRP):
        pl.semaphore_signal(barrier, inc=1, device_id=((grp + o) % N_GRP, me), device_id_type=MESH)

    def copy(src, dst, send, got, g, to):
        pltpu.make_async_remote_copy(src, dst, send, recv.at[got], device_id=(g, to), device_id_type=MESH).start()

    def blocks(ref, n, lo, count):
        return ref.at[pl.ds(lo * n, count * n), :]

    def spread_u(ref, n, send, got):
        for du in (1, 3, 2):
            copy(blocks(ref, n, 0, 1), blocks(ref, n, 4 - du, 1), send, got, grp, at(du, 0))

    def spread_v(ref, n, lo, count, send, got):
        for dv in (1, 3, 2):
            copy(blocks(ref, n, lo, count), blocks(ref, n, 4 * (4 - dv) + lo, count), send, got, grp, at(0, dv))

    def spread_sib(ref, n, lo, count, send, got):
        copy(blocks(ref, n, lo, count), blocks(ref, n, 16 + lo, count), send, got, grp, sib)

    def done(ref, n, count, sem):
        part = blocks(ref, n, 0, count)
        pltpu.make_async_copy(part, part, sem).wait()

    positions = send_pos[0].astype(F32)
    pos[0:16, 0:SLOT] = positions[0:16].astype(BF16)
    pos[0:16, SLOT:128] = positions[16:32].astype(BF16)
    owner, rank = hub_owner_rank(hub_ids[...])
    local = hub_ids[...] - (grp * N_DEV + me) * NPD
    node_in.wait()
    pick = jnp.where(lax.broadcasted_iota(I32, (NPD, BND), 0) == bnd_idx[...], 1.0, 0.0).astype(BF16)
    bnd[0:BND, :] = dot(pick, node[...], TN).astype(BF16)
    pick = jnp.where(lax.broadcasted_iota(I32, (NPD, HUBS), 0) == local, 1.0, 0.0).astype(BF16)
    rows = dot(pick, node[...], TN).astype(BF16)
    by_rank = jnp.where(lax.broadcasted_iota(I32, (8, HUBS), 0) == rank, 1.0, 0.0).astype(BF16)
    pair = dot(by_rank, rows)
    tile = jnp.concatenate([pair[0:2, q * 128 : (q + 1) * 128] for q in range(8)], axis=0)
    tile_z[0] = tile.astype(BF16)

    pl.semaphore_wait(barrier, 7 + N_GRP - 1)

    spread_u(bnd, BND, b_send, 0)
    spread_u(pos, 16, p_send, 1)
    for o in range(1, N_GRP):
        copy(tile_z.at[0], tile_z.at[o], z_send, 2, (grp + o) % N_GRP, me)
    spread_sib(bnd, BND, 0, 1, b_sib_send, 3)

    col = edge_column(edge_src[...], me)
    third = lambda n: (n * 43) >> 7
    own = col - HALO
    hub = own - NPD
    halo_digit, own_digit = third(col >> 6), third(own >> 5)
    line = jnp.where(own < 0, col - HALO_LINES * halo_digit,
                     jnp.where(hub < 0, HALO_LINES + own - OWN_LINES * own_digit, HUB_AT + (hub & 7)))
    shift = jnp.where(own < 0, HALO_BITS * halo_digit, OWN_BITS * jnp.where(hub < 0, own_digit, hub >> 3))
    line_of[...] = line
    weight_of[...] = jnp.left_shift(jnp.ones_like(shift), shift).astype(F32)

    def make(step):
        one_dst, one_src = ((one_dst_a, one_src_a), (one_dst_b, one_src_b))[step % 2]
        zero, one = jnp.zeros((), BF16), jnp.ones((), BF16)
        for r in range(STEP_ROWS):
            row = step * STEP_ROWS + r
            here = slice(r * 128, (r + 1) * 128)
            d = edge_dst[row : row + 1, :].astype(I16)
            s = line_of[row : row + 1, :].astype(I16)
            w = weight_of[row : row + 1, :].astype(BF16)
            one_dst[:, here] = jnp.where(lax.broadcasted_iota(I16, (NPD, 128), 0) == d, one, zero)
            lines = lax.broadcasted_iota(I16, (LINES, 128), 0)
            value = jnp.where(lines == s, jnp.broadcast_to(w, (LINES, 128)), zero)
            one_src[:, here] = jnp.where(lines >= DEGREE_AT, one, value)

    def add(step):
        one_dst, one_src = ((one_dst_a, one_src_a), (one_dst_b, one_src_b))[step % 2]
        part = dot(one_src[...], one_dst[...], NT)
        packed[...] = part if step == 0 else packed[...] + part

    make(0)
    spread_v(bnd, BND, 0, 1, b_send, 4)
    make(1)
    add(0)

    done(bnd, BND, 3, recv.at[0])
    spread_v(bnd, BND, 1, 3, b_send, 5)
    spread_sib(bnd, BND, 1, 3, b_sib_send, 3)
    done(pos, 16, 3, recv.at[1])
    spread_v(pos, 16, 0, 4, p_send, 6)
    part = tile_z.at[pl.ds(1, N_GRP - 1)]
    pltpu.make_async_copy(part, part, recv.at[2]).wait()
    tiles = [tile_z[o].astype(F32) for o in range(N_GRP)]
    for q in range(8):
        rows = jnp.concatenate([t[2 * q : 2 * q + 2, :] for t in tiles], axis=0)
        column[0:COLUMN, q * 128 : (q + 1) * 128] = rows.astype(BF16)
    spread_u(column, COLUMN, h_send, 7)

    make(2)
    add(1)
    make(3)
    add(2)
    add(3)

    done(column, COLUMN, 3, recv.at[7])
    spread_v(column, COLUMN, 0, 4, h_send, 8)
    spread_sib(column, COLUMN, 0, 4, h_sib_send, 9)
    done(pos, 16, 12, recv.at[6])
    spread_sib(pos, 16, 0, 16, p_sib_send, 10)

    total = jnp.zeros((1, NPD), I32)
    ints = packed[0:HALO_LINES, :].astype(I32)
    for i in range(HALO_DIGITS):
        digit = ints >> (HALO_BITS * i)
        if i < HALO_DIGITS - 1:
            digit = digit & (2**HALO_BITS - 1)
        total = total + jnp.sum(digit, axis=0, keepdims=True)
        halo_cnt[i * HALO_LINES : (i + 1) * HALO_LINES, :] = digit.astype(F32).astype(BF16)
    ints = packed[HALO_LINES:DEGREE_AT, :].astype(I32)
    hub_parts = []
    for i in range(OWN_DIGITS):
        digit = ints >> (OWN_BITS * i)
        if i < OWN_DIGITS - 1:
            digit = digit & (2**OWN_BITS - 1)
        total = total + jnp.sum(digit, axis=0, keepdims=True)
        digit = digit.astype(F32)
        own_cnt[i * OWN_LINES : (i + 1) * OWN_LINES, :] = digit[0:OWN_LINES].astype(BF16)
        hub_parts.append(digit[OWN_LINES:])
    own_cnt[NPD : NPD + HUBS, :] = jnp.concatenate(hub_parts, axis=0).astype(BF16)
    degree = packed[DEGREE_AT : DEGREE_AT + 1, :]
    largest = jnp.max(packed[0:DEGREE_AT, :], axis=0, keepdims=True)
    bad = (total != degree.astype(I32)) | (largest >= LIMIT) | (degree > 256.0)
    flag[...] = jnp.broadcast_to(jnp.max(jnp.where(bad, 1, 0), axis=1, keepdims=True), (8, 128))
    inverse = jnp.transpose(jnp.broadcast_to(1.0 / degree, (128, NPD)))
    inverse = jnp.concatenate([inverse] * 8, axis=1)

    def third_of(i):
        return slice(i * 256, (i + 1) * 256)

    ws_in.wait()
    for i in range(3):
        acc[third_of(i), :] = dot(node[third_of(i), :], ws[...])

    done(bnd, BND, 3, recv.at[4])
    done(bnd, BND, 9, recv.at[5])
    spread_sib(bnd, BND, 4, 12, b_sib_send, 11)

    for i in range(3):
        summed[third_of(i), :] = dot(own_cnt[0:NPD, third_of(i)], node[...], TN)

    done(column, COLUMN, 12, recv.at[8])
    spread_sib(column, COLUMN, 4, 12, h_sib_send, 9)

    done(pos, 16, 16, recv.at[10])
    every = pos[...].astype(F32).reshape(N_DEV, 16, 128)
    mine = lax.broadcasted_iota(I32, (N_DEV, 16, 128), 1) == me % 16
    rows = jnp.sum(jnp.where(mine, every, 0.0), axis=1)
    turned = pltpu.roll(rows, SLOT, 1)
    low = jnp.where(me < 16, rows, turned)
    high = jnp.where(me < 16, turned, rows)
    lane = lax.broadcasted_iota(I32, (128, 128), 1)
    line = lax.broadcasted_iota(I32, (128, 128), 0)
    for g in range(8):
        for half in range(2):
            a = 4 * g + 2 * half
            wanted = jnp.where(lane < SLOT, low[a : a + 1, :], high[a + 1 : a + 2, :]).astype(I32)
            match = ((line >> 5) == 2 * half + (lane >> 6)) & ((line & 31) == wanted)
            remap[g * 128 : (g + 1) * 128, half * 128 : (half + 1) * 128] = jnp.where(match, 1.0, 0.0).astype(BF16)
    for g in range(8):
        part = dot(remap[g * 128 : (g + 1) * 128, :], halo_cnt[g * 256 : (g + 1) * 256, :])
        bnd_cnt[g * 128 : (g + 1) * 128, :] = part.astype(BF16)

    done(bnd, BND, 4, recv.at[3])
    done(bnd, BND, 12, recv.at[11])
    bnd_out = pltpu.make_async_copy(bnd, bnd_hbm, out_sem.at[0])
    bnd_out.start()
    for i in range(3):
        summed[third_of(i), :] += dot(bnd_cnt[:, third_of(i)], bnd[...], TN)

    done(column, COLUMN, 16, recv.at[9])
    at_row = place(owner % N_DEV, me) * COLUMN + ((grp - owner // N_DEV) & 7) * 2 + rank
    choose = jnp.where(lax.broadcasted_iota(I32, (N_DEV * COLUMN, HUBS), 0) == at_row, 1.0, 0.0).astype(BF16)
    hubs[...] = dot(choose, column[...], TN).astype(BF16)
    hubs_out = pltpu.make_async_copy(hubs, hubs_hbm, out_sem.at[1])
    hubs_out.start()
    remap_out = pltpu.make_async_copy(remap, remap_hbm, out_sem.at[2])
    remap_out.start()

    wn_in.wait()
    for i in range(3):
        total = summed[third_of(i), :] + dot(own_cnt[NPD : NPD + HUBS, third_of(i)], hubs[...], TN)
        mean = (total * inverse[third_of(i), :]).astype(BF16)
        mixed = acc[third_of(i), :] + dot(mean, wn[...])
        out_buf[third_of(i), :] = jnp.maximum(mixed, 0.0).astype(BF16)
        pltpu.make_async_copy(out_buf.at[third_of(i), :], out_hbm.at[third_of(i), :], out_sem.at[3]).start()

    done(bnd, BND, 15, b_send)
    done(bnd, BND, 16, b_sib_send)
    done(pos, 16, 15, p_send)
    done(pos, 16, 16, p_sib_send)
    done(column, COLUMN, 15, h_send)
    done(column, COLUMN, 16, h_sib_send)
    part = tile_z.at[pl.ds(1, N_GRP - 1)]
    pltpu.make_async_copy(part, part, z_send).wait()
    bnd_out.wait()
    hubs_out.wait()
    remap_out.wait()
    pltpu.make_async_copy(out_buf, out_hbm, out_sem.at[3]).wait()


def finish_kernel(flag, fast_hbm, node_hbm, ws_hbm, wn_hbm, bnd_hbm, hubs_hbm, remap_hbm, edge_src, edge_dst,
                  out_hbm,
                  node, ws, wn, bnd, hubs, remap, one_dst, one_src, col_of, summed, degree, out_buf, sem):
    me = lax.axis_index("dev")

    @pl.when(flag[0, 0] == 0)
    def _():
        parts = [pl.ds(i * 192, 192) for i in range(4)]
        ins = [pltpu.make_async_copy(fast_hbm.at[p, :], out_buf.at[p, :], sem.at[i]) for i, p in enumerate(parts)]
        outs = [pltpu.make_async_copy(out_buf.at[p, :], out_hbm.at[p, :], sem.at[4 + i]) for i, p in enumerate(parts)]
        for one in ins:
            one.start()
        for one, two in zip(ins, outs):
            one.wait()
            two.start()
        for two in outs:
            two.wait()

    @pl.when(flag[0, 0] != 0)
    def _():
        pairs = [(node_hbm, node), (ws_hbm, ws), (wn_hbm, wn), (bnd_hbm, bnd), (hubs_hbm, hubs), (remap_hbm, remap)]
        copies = [pltpu.make_async_copy(a, b, sem.at[i]) for i, (a, b) in enumerate(pairs)]
        for one in copies:
            one.start()
        for one in copies:
            one.wait()
        col_of[...] = edge_column(edge_src[...], me)
        degree[...] = jnp.zeros_like(degree)
        summed[...] = jnp.zeros_like(summed)

        @pl.loop(0, ROWS)
        def _(r):
            here = pl.ds(pl.multiple_of(r * 128, 128), 128)
            match = lax.broadcasted_iota(I32, (NPD, 128), 0) == edge_dst[pl.ds(r, 1), :]
            hit = jnp.where(match, 1.0, 0.0)
            one_dst[:, here] = hit.astype(BF16)
            degree[...] += jnp.sum(hit, axis=1, keepdims=True)

        def block(first, rows):
            n = rows.shape[0]

            @pl.loop(0, ROWS)
            def _(r):
                here = pl.ds(pl.multiple_of(r * 128, 128), 128)
                match = lax.broadcasted_iota(I32, (256, 128), 0) + first == col_of[pl.ds(r, 1), :]
                one_src[:, here] = jnp.where(match, 1.0, 0.0).astype(BF16)

            count = jnp.zeros((NPD, 256), F32)
            for i in range(STEPS):
                here = slice(i * STEP, (i + 1) * STEP)
                count = count + dot(one_dst[:, here], one_src[:, here], NT)
            upper = jnp.floor(count * (1.0 / 256.0)) * 256.0
            lower = count - upper
            summed[...] += dot(upper[:, 0:n].astype(BF16), rows) + dot(lower[:, 0:n].astype(BF16), rows)

        @pl.loop(0, 8)
        def _(g):
            lines = pl.ds(pl.multiple_of(g * 128, 128), 128)
            block(g * 256, dot(remap[lines, :], bnd[lines, :], TN).astype(BF16))

        @pl.loop(0, 3)
        def _(g):
            block(HALO + g * 256, node[pl.ds(pl.multiple_of(g * 256, 256), 256), :])

        block(HALO + NPD, hubs[...])
        mean = (summed[...] / degree[...]).astype(BF16)
        mixed = dot(node[...], ws[...]) + dot(mean, wn[...])
        out_buf[...] = jnp.maximum(mixed, 0.0).astype(BF16)
        last = pltpu.make_async_copy(out_buf, out_hbm, sem.at[0])
        last.start()
        last.wait()


def body(node_rows, w_self, w_neigh, hub_ids, bnd_idx, send_pos, edge_src, edge_dst):
    any_, vmem = pl.BlockSpec(memory_space=pl.ANY), pl.BlockSpec(memory_space=pltpu.VMEM)
    dma = pltpu.SemaphoreType.DMA
    src, dst = edge_src.reshape(ROWS, 128), edge_dst.reshape(ROWS, 128)
    scratch = [
        pltpu.VMEM((NPD, D), BF16),
        pltpu.VMEM((D, D), BF16),
        pltpu.VMEM((D, D), BF16),
        pltpu.VMEM((N_DEV * BND, D), BF16),
        pltpu.VMEM((N_DEV * 16, 128), BF16),
        pltpu.VMEM((N_DEV * COLUMN, D), BF16),
        pltpu.VMEM((HUBS, D), BF16),
        pltpu.VMEM((N_GRP, 16, 128), BF16),
        pltpu.VMEM((N_DEV * BND, 256), BF16),
        pltpu.VMEM((ROWS, 128), I32),
        pltpu.VMEM((ROWS, 128), F32),
        pltpu.VMEM((NPD, STEP), BF16),
        pltpu.VMEM((NPD, STEP), BF16),
        pltpu.VMEM((LINES, STEP), BF16),
        pltpu.VMEM((LINES, STEP), BF16),
        pltpu.VMEM((LINES, NPD), F32),
        pltpu.VMEM((HALO_DIGITS * HALO_LINES, NPD), BF16),
        pltpu.VMEM((NPD + HUBS, NPD), BF16),
        pltpu.VMEM((N_DEV * BND, NPD), BF16),
        pltpu.VMEM((NPD, D), F32),
        pltpu.VMEM((NPD, D), F32),
        pltpu.VMEM((NPD, D), BF16),
        dma((3,)), dma((4,)), dma, dma, dma, dma, dma, dma, dma, dma((12,)),
    ]
    outs = [
        jax.ShapeDtypeStruct((NPD, D), BF16),
        jax.ShapeDtypeStruct((N_DEV * BND, D), BF16),
        jax.ShapeDtypeStruct((HUBS, D), BF16),
        jax.ShapeDtypeStruct((N_DEV * BND, 256), BF16),
        jax.ShapeDtypeStruct((8, 128), I32),
    ]
    fast, bnd, hubs, remap, flag = pl.pallas_call(
        main_kernel,
        out_shape=outs,
        in_specs=[any_, any_, any_, vmem, vmem, vmem, vmem, vmem],
        out_specs=[any_, any_, any_, any_, vmem],
        scratch_shapes=scratch,
        compiler_params=pltpu.CompilerParams(
            collective_id=0, has_side_effects=True, vmem_limit_bytes=56 * 2**20
        ),
        name="sage_main",
    )(node_rows, w_self, w_neigh, hub_ids.reshape(1, HUBS), bnd_idx, send_pos, src, dst)
    scratch = [
        pltpu.VMEM((NPD, D), BF16),
        pltpu.VMEM((D, D), BF16),
        pltpu.VMEM((D, D), BF16),
        pltpu.VMEM((N_DEV * BND, D), BF16),
        pltpu.VMEM((HUBS, D), BF16),
        pltpu.VMEM((N_DEV * BND, 256), BF16),
        pltpu.VMEM((NPD, E_DEV), BF16),
        pltpu.VMEM((256, E_DEV), BF16),
        pltpu.VMEM((ROWS, 128), I32),
        pltpu.VMEM((NPD, D), F32),
        pltpu.VMEM((NPD, 1), F32),
        pltpu.VMEM((NPD, D), BF16),
        dma((8,)),
    ]
    return pl.pallas_call(
        finish_kernel,
        out_shape=jax.ShapeDtypeStruct((NPD, D), BF16),
        in_specs=[pl.BlockSpec(memory_space=pltpu.SMEM)] + [any_] * 7 + [vmem, vmem],
        out_specs=any_,
        scratch_shapes=scratch,
        compiler_params=pltpu.CompilerParams(vmem_limit_bytes=56 * 2**20),
        name="sage_finish",
    )(flag, fast, node_rows, w_self, w_neigh, bnd, hubs, remap, src, dst)


def solution(mesh):
    in_specs = (
        P(("grp", "dev"), None),
        P(),
        P(),
        P(),
        P(("grp", "dev"), None),
        P(("grp", "dev"), None, None),
        P(("grp", "dev")),
        P(("grp", "dev")),
    )
    out_specs = P(("grp", "dev"), None)
    return jax.shard_map(body, mesh=mesh, in_specs=in_specs, out_specs=out_specs, check_vma=False)
```

time: 329 us -> 43 us (0.13)
  waiting for transfers between devices: 205 us -> 0 us
  Pallas kernels: 0 us -> 42.6 us
  other arithmetic: 42.5 us -> 0 us
  local copies, waits for them, and re-layouts: 38.2 us -> 0 us
  matrix products: 19.4 us -> 0 us
  between operations: 13.5 us -> 0.17 us
  starting transfers between devices: 8.83 us -> 0 us
    pmax x1 -> x0, waiting for transfers between devices: 205 us -> none  [body(): hub_rows = lax.pmax(masked, ('grp', 'dev'))]
    pallas_call x0 -> x2, Pallas kernels: none -> 42.6 us  [the longest x1 39.7 us: body(): pl.pallas_call(main_kernel, out_shape=outs, in_specs=[any_, any_, any_, v...]
    unnamed x4 -> x0, other arithmetic: 36.8 us -> none
    gather x4 -> x0, local copies, waits for them, and re-layouts: 27.7 us -> none  [the longest x3 25.3 us: body(): outgoing = node_rows[bnd_idx[0][send_pos[0]]]]
    dot_general x2 -> x0, matrix products: 19.4 us -> none  [the longest x1 14.6 us: body(): jnp.dot(neighbour_mean, w_neigh, preferred_element_type=jnp.float32)]
    scatter-add x1 -> x0, local copies, waits for them, and re-layouts: 10.4 us -> none  [body(): jnp.zeros((NPD, table_rows), jnp.float32).at[edge_dst, edge_src].add(1.0)]
    all_to_all x1 -> x0, starting transfers between devices: 8.79 us -> none  [body(): lax.all_to_all(outgoing, 'dev', split_axis=0, concat_axis=0, tiled=True)]
    reduce_sum x1 -> x0, other arithmetic: 4.07 us -> none  [body(): degree = jnp.sum(counts, axis=1)]
  transfers between devices with their start and end apart: 2 -> 0, of which waited for: 1 -> 0; matrix products, arithmetic and copies ran while one was open for 18% -> 0% of each run, Pallas kernels for 0% -> 0%
where the time goes in v2:
time: 43 us; the launch traced here: 42.8 us
  Pallas kernels  42.6 us (99%)
    pallas_call x1, Pallas kernels, body(): pl.pallas_call(main_kernel, out_shape=outs, in_specs=[any_, any_, any_, v...  39.7 us
    pallas_call x1, Pallas kernels, body(): pl.pallas_call(finish_kernel, out_shape=jax.ShapeDtypeStruct((NPD, D), BF...  2.97 us

profile of v2, /device:TPU:1, one launch (start us, length us, event | category | flops | bytes accessed | tf_op | source)
XLA Modules:
  0.0 42.8 jit_solution(17451714204052130084)
XLA Ops:
  0.0 39.7 %sage_main.1 = (bf16[768,1024]{1,0:T(8,128)(2,1)}, bf16[1024,1024]{1,0:T(8,128)(2,1)}, bf16[64,1024]{1,0:T(8,128)(2,1)}, bf16[1024,256]{1,0:T(8,128)(2,1)}, s32[8,128]{1,0:T(8,128)}) custom-call(bf16[768,1024]{1,0:T(8,128)(2,1)} %node_hbm.3, bf16[1024,1024]{1,0:T(8,128)(2,1)} %ws_hbm.3, bf16[1024,1024]{1,0:T(8,128)(2,1)} %wn_hbm.3, s32[1,64]{1,0:T(1,128)} %bitcast.7, ...), custom_call_target="tpu_custom_call" | custom-call | tf_op jit(solution)/shard_map/sage_main/pallas_call | solution.py:405
  39.7 3.0 %sage_finish.1 = bf16[768,1024]{1,0:T(8,128)(2,1)} custom-call(s32[8,128]{1,0:T(8,128)} %get-tuple-element.10.flag, bf16[768,1024]{1,0:T(8,128)(2,1)} %get-tuple-element.11.fast_hbm, bf16[768,1024]{1,0:T(8,128)(2,1)} %node_hbm.3, bf16[1024,1024]{1,0:T(8,128)(2,1)} %ws_hbm.3, bf16[1024,1024]{1,0:T(8,128)(2,1)} %wn_hbm.3, ...), custom_call_target="tpu_custom_call" | custom-call | tf_op jit(solution)/shard_map/sage_finish/pallas_call | solution.py:431

commit v3 on v2

--- a/solution.py
+++ b/solution.py
@@ -62,10 +62,10 @@
 
 
 def main_kernel(node_hbm, ws_hbm, wn_hbm, hub_ids, bnd_idx, send_pos, edge_src, edge_dst,
-                out_hbm, bnd_hbm, hubs_hbm, remap_hbm, flag,
-                node, ws, wn, bnd, pos, column, hubs, tile_z, remap,
-                line_of, weight_of, one_dst_a, one_dst_b, one_src_a, one_src_b, packed,
-                halo_cnt, own_cnt, bnd_cnt, acc, summed, out_buf,
+                out_hbm, bnd_hbm, column_hbm, remap_hbm, flag,
+                node, ws, wn, bnd, pos, column, tile_z, remap,
+                line_of, weight_of, one_dst, one_src, packed, inverse,
+                halo_cnt, own_cnt, hub_cnt, column_cnt, bnd_cnt, acc, summed, out_buf,
                 in_sem, out_sem, b_send, b_sib_send, p_send, p_sib_send, h_send, h_sib_send, z_send, recv):
     grp = lax.axis_index("grp")
     me = lax.axis_index("dev")
@@ -89,6 +89,8 @@
     for o in range(1, N_GRP):
         pl.semaphore_signal(barrier, inc=1, device_id=((grp + o) % N_GRP, me), device_id_type=MESH)
 
+    packed[...] = jnp.zeros_like(packed)
+
     def copy(src, dst, send, got, g, to):
         pltpu.make_async_remote_copy(src, dst, send, recv.at[got], device_id=(g, to), device_id_type=MESH).start()
 
@@ -110,28 +112,20 @@
         part = blocks(ref, n, 0, count)
         pltpu.make_async_copy(part, part, sem).wait()
 
+    owner, rank = hub_owner_rank(hub_ids[...])
+    local = hub_ids[...] - (grp * N_DEV + me) * NPD
+    wanted = jnp.concatenate([local, bnd_idx[...]], axis=1)
+    pick = jnp.where(lax.broadcasted_iota(I32, (NPD, HUBS + BND), 0) == wanted, 1.0, 0.0).astype(BF16)
+    by_rank = jnp.where(lax.broadcasted_iota(I32, (8, HUBS), 0) == rank, 1.0, 0.0).astype(BF16)
     positions = send_pos[0].astype(F32)
     pos[0:16, 0:SLOT] = positions[0:16].astype(BF16)
     pos[0:16, SLOT:128] = positions[16:32].astype(BF16)
-    owner, rank = hub_owner_rank(hub_ids[...])
-    local = hub_ids[...] - (grp * N_DEV + me) * NPD
     node_in.wait()
-    pick = jnp.where(lax.broadcasted_iota(I32, (NPD, BND), 0) == bnd_idx[...], 1.0, 0.0).astype(BF16)
-    bnd[0:BND, :] = dot(pick, node[...], TN).astype(BF16)
-    pick = jnp.where(lax.broadcasted_iota(I32, (NPD, HUBS), 0) == local, 1.0, 0.0).astype(BF16)
     rows = dot(pick, node[...], TN).astype(BF16)
-    by_rank = jnp.where(lax.broadcasted_iota(I32, (8, HUBS), 0) == rank, 1.0, 0.0).astype(BF16)
-    pair = dot(by_rank, rows)
+    bnd[0:BND, :] = rows[HUBS:]
+    pair = dot(by_rank, rows[0:HUBS])
     tile = jnp.concatenate([pair[0:2, q * 128 : (q + 1) * 128] for q in range(8)], axis=0)
     tile_z[0] = tile.astype(BF16)
-
-    pl.semaphore_wait(barrier, 7 + N_GRP - 1)
-
-    spread_u(bnd, BND, b_send, 0)
-    spread_u(pos, 16, p_send, 1)
-    for o in range(1, N_GRP):
-        copy(tile_z.at[0], tile_z.at[o], z_send, 2, (grp + o) % N_GRP, me)
-    spread_sib(bnd, BND, 0, 1, b_sib_send, 3)
 
     col = edge_column(edge_src[...], me)
     third = lambda n: (n * 43) >> 7
@@ -144,54 +138,36 @@
     line_of[...] = line
     weight_of[...] = jnp.left_shift(jnp.ones_like(shift), shift).astype(F32)
 
-    def make(step):
-        one_dst, one_src = ((one_dst_a, one_src_a), (one_dst_b, one_src_b))[step % 2]
+    distance = jnp.minimum(grp, N_GRP - grp)
+    first_send = jnp.maximum(2 - distance, 0)
+
+    @pl.loop(0, STEPS)
+    def _(step):
+        @pl.when(step == first_send)
+        def _():
+            pl.semaphore_wait(barrier, 7 + N_GRP - 1)
+            for o in range(1, N_GRP):
+                copy(tile_z.at[0], tile_z.at[o], z_send, 2, (grp + o) % N_GRP, me)
+            spread_u(bnd, BND, b_send, 0)
+            spread_u(pos, 16, p_send, 1)
+            spread_sib(bnd, BND, 0, 1, b_sib_send, 3)
+
         zero, one = jnp.zeros((), BF16), jnp.ones((), BF16)
         for r in range(STEP_ROWS):
-            row = step * STEP_ROWS + r
+            row = pl.ds(step * STEP_ROWS + r, 1)
             here = slice(r * 128, (r + 1) * 128)
-            d = edge_dst[row : row + 1, :].astype(I16)
-            s = line_of[row : row + 1, :].astype(I16)
-            w = weight_of[row : row + 1, :].astype(BF16)
+            d = edge_dst[row, :].astype(I16)
+            s = line_of[row, :].astype(I16)
+            w = weight_of[row, :].astype(BF16)
             one_dst[:, here] = jnp.where(lax.broadcasted_iota(I16, (NPD, 128), 0) == d, one, zero)
             lines = lax.broadcasted_iota(I16, (LINES, 128), 0)
             value = jnp.where(lines == s, jnp.broadcast_to(w, (LINES, 128)), zero)
             one_src[:, here] = jnp.where(lines >= DEGREE_AT, one, value)
-
-    def add(step):
-        one_dst, one_src = ((one_dst_a, one_src_a), (one_dst_b, one_src_b))[step % 2]
-        part = dot(one_src[...], one_dst[...], NT)
-        packed[...] = part if step == 0 else packed[...] + part
-
-    make(0)
-    spread_v(bnd, BND, 0, 1, b_send, 4)
-    make(1)
-    add(0)
-
-    done(bnd, BND, 3, recv.at[0])
-    spread_v(bnd, BND, 1, 3, b_send, 5)
-    spread_sib(bnd, BND, 1, 3, b_sib_send, 3)
-    done(pos, 16, 3, recv.at[1])
-    spread_v(pos, 16, 0, 4, p_send, 6)
-    part = tile_z.at[pl.ds(1, N_GRP - 1)]
-    pltpu.make_async_copy(part, part, recv.at[2]).wait()
-    tiles = [tile_z[o].astype(F32) for o in range(N_GRP)]
-    for q in range(8):
-        rows = jnp.concatenate([t[2 * q : 2 * q + 2, :] for t in tiles], axis=0)
-        column[0:COLUMN, q * 128 : (q + 1) * 128] = rows.astype(BF16)
-    spread_u(column, COLUMN, h_send, 7)
-
-    make(2)
-    add(1)
-    make(3)
-    add(2)
-    add(3)
-
-    done(column, COLUMN, 3, recv.at[7])
-    spread_v(column, COLUMN, 0, 4, h_send, 8)
-    spread_sib(column, COLUMN, 0, 4, h_sib_send, 9)
-    done(pos, 16, 12, recv.at[6])
-    spread_sib(pos, 16, 0, 16, p_sib_send, 10)
+        packed[...] += dot(one_src[...], one_dst[...], NT)
+
+        @pl.when(step == first_send)
+        def _():
+            spread_v(bnd, BND, 0, 1, b_send, 4)
 
     total = jnp.zeros((1, NPD), I32)
     ints = packed[0:HALO_LINES, :].astype(I32)
@@ -211,30 +187,48 @@
         digit = digit.astype(F32)
         own_cnt[i * OWN_LINES : (i + 1) * OWN_LINES, :] = digit[0:OWN_LINES].astype(BF16)
         hub_parts.append(digit[OWN_LINES:])
-    own_cnt[NPD : NPD + HUBS, :] = jnp.concatenate(hub_parts, axis=0).astype(BF16)
+    hub_cnt[...] = jnp.concatenate(hub_parts, axis=0).astype(BF16)
+
     degree = packed[DEGREE_AT : DEGREE_AT + 1, :]
     largest = jnp.max(packed[0:DEGREE_AT, :], axis=0, keepdims=True)
     bad = (total != degree.astype(I32)) | (largest >= LIMIT) | (degree > 256.0)
     flag[...] = jnp.broadcast_to(jnp.max(jnp.where(bad, 1, 0), axis=1, keepdims=True), (8, 128))
-    inverse = jnp.transpose(jnp.broadcast_to(1.0 / degree, (128, NPD)))
-    inverse = jnp.concatenate([inverse] * 8, axis=1)
+    inverse[...] = jnp.transpose(jnp.broadcast_to(1.0 / degree, (128, NPD)))
 
     def third_of(i):
         return slice(i * 256, (i + 1) * 256)
+
+    done(bnd, BND, 3, recv.at[0])
+    spread_v(bnd, BND, 1, 3, b_send, 5)
+    done(pos, 16, 3, recv.at[1])
+    spread_v(pos, 16, 0, 4, p_send, 6)
+    spread_sib(bnd, BND, 1, 3, b_sib_send, 3)
 
     ws_in.wait()
     for i in range(3):
         acc[third_of(i), :] = dot(node[third_of(i), :], ws[...])
 
-    done(bnd, BND, 3, recv.at[4])
-    done(bnd, BND, 9, recv.at[5])
-    spread_sib(bnd, BND, 4, 12, b_sib_send, 11)
-
     for i in range(3):
         summed[third_of(i), :] = dot(own_cnt[0:NPD, third_of(i)], node[...], TN)
 
-    done(column, COLUMN, 12, recv.at[8])
-    spread_sib(column, COLUMN, 4, 12, h_sib_send, 9)
+    part = tile_z.at[pl.ds(1, N_GRP - 1)]
+    pltpu.make_async_copy(part, part, recv.at[2]).wait()
+    tiles = [tile_z[o].astype(F32) for o in range(N_GRP)]
+    for q in range(8):
+        rows = jnp.concatenate([t[2 * q : 2 * q + 2, :] for t in tiles], axis=0)
+        column[0:COLUMN, q * 128 : (q + 1) * 128] = rows.astype(BF16)
+    spread_u(column, COLUMN, h_send, 7)
+
+    done(pos, 16, 12, recv.at[6])
+    spread_sib(pos, 16, 0, 16, p_sib_send, 10)
+
+    at_row = place(owner % N_DEV, me) * COLUMN + ((grp - owner // N_DEV) & 7) * 2 + rank
+    choose = jnp.where(lax.broadcasted_iota(I32, (N_DEV * COLUMN, HUBS), 0) == at_row, 1.0, 0.0).astype(BF16)
+    column_cnt[...] = dot(choose, hub_cnt[...]).astype(BF16)
+
+    done(column, COLUMN, 3, recv.at[7])
+    spread_v(column, COLUMN, 0, 4, h_send, 8)
+    spread_sib(column, COLUMN, 0, 4, h_sib_send, 9)
 
     done(pos, 16, 16, recv.at[10])
     every = pos[...].astype(F32).reshape(N_DEV, 16, 128)
@@ -254,27 +248,32 @@
     for g in range(8):
         part = dot(remap[g * 128 : (g + 1) * 128, :], halo_cnt[g * 256 : (g + 1) * 256, :])
         bnd_cnt[g * 128 : (g + 1) * 128, :] = part.astype(BF16)
+    remap_out = pltpu.make_async_copy(remap, remap_hbm, out_sem.at[2])
+    remap_out.start()
+
+    done(bnd, BND, 3, recv.at[4])
+    done(bnd, BND, 9, recv.at[5])
+    spread_sib(bnd, BND, 4, 12, b_sib_send, 11)
+    for i in range(3):
+        summed[third_of(i), :] += dot(bnd_cnt[0:512, third_of(i)], bnd[0:512, :], TN)
+
+    done(column, COLUMN, 12, recv.at[8])
+    spread_sib(column, COLUMN, 4, 12, h_sib_send, 9)
 
     done(bnd, BND, 4, recv.at[3])
     done(bnd, BND, 12, recv.at[11])
     bnd_out = pltpu.make_async_copy(bnd, bnd_hbm, out_sem.at[0])
     bnd_out.start()
     for i in range(3):
-        summed[third_of(i), :] += dot(bnd_cnt[:, third_of(i)], bnd[...], TN)
-
+        summed[third_of(i), :] += dot(bnd_cnt[512:, third_of(i)], bnd[512:, :], TN)
+
+    wn_in.wait()
     done(column, COLUMN, 16, recv.at[9])
-    at_row = place(owner % N_DEV, me) * COLUMN + ((grp - owner // N_DEV) & 7) * 2 + rank
-    choose = jnp.where(lax.broadcasted_iota(I32, (N_DEV * COLUMN, HUBS), 0) == at_row, 1.0, 0.0).astype(BF16)
-    hubs[...] = dot(choose, column[...], TN).astype(BF16)
-    hubs_out = pltpu.make_async_copy(hubs, hubs_hbm, out_sem.at[1])
-    hubs_out.start()
-    remap_out = pltpu.make_async_copy(remap, remap_hbm, out_sem.at[2])
-    remap_out.start()
-
-    wn_in.wait()
+    column_out = pltpu.make_async_copy(column, column_hbm, out_sem.at[1])
+    column_out.start()
     for i in range(3):
-        total = summed[third_of(i), :] + dot(own_cnt[NPD : NPD + HUBS, third_of(i)], hubs[...], TN)
-        mean = (total * inverse[third_of(i), :]).astype(BF16)
+        total = summed[third_of(i), :] + dot(column_cnt[:, third_of(i)], column[...], TN)
+        mean = (total * jnp.concatenate([inverse[third_of(i), :]] * 8, axis=1)).astype(BF16)
         mixed = acc[third_of(i), :] + dot(mean, wn[...])
         out_buf[third_of(i), :] = jnp.maximum(mixed, 0.0).astype(BF16)
         pltpu.make_async_copy(out_buf.at[third_of(i), :], out_hbm.at[third_of(i), :], out_sem.at[3]).start()
@@ -288,37 +287,44 @@
     part = tile_z.at[pl.ds(1, N_GRP - 1)]
     pltpu.make_async_copy(part, part, z_send).wait()
     bnd_out.wait()
-    hubs_out.wait()
+    column_out.wait()
     remap_out.wait()
     pltpu.make_async_copy(out_buf, out_hbm, out_sem.at[3]).wait()
 
 
-def finish_kernel(flag, fast_hbm, node_hbm, ws_hbm, wn_hbm, bnd_hbm, hubs_hbm, remap_hbm, edge_src, edge_dst,
+def finish_kernel(flag_hbm, fast_hbm, node_hbm, ws_hbm, wn_hbm, bnd_hbm, column_hbm, remap_hbm, hub_hbm, src_hbm, dst_hbm,
                   out_hbm,
-                  node, ws, wn, bnd, hubs, remap, one_dst, one_src, col_of, summed, degree, out_buf, sem):
-    me = lax.axis_index("dev")
-
-    @pl.when(flag[0, 0] == 0)
-    def _():
-        parts = [pl.ds(i * 192, 192) for i in range(4)]
-        ins = [pltpu.make_async_copy(fast_hbm.at[p, :], out_buf.at[p, :], sem.at[i]) for i, p in enumerate(parts)]
-        outs = [pltpu.make_async_copy(out_buf.at[p, :], out_hbm.at[p, :], sem.at[4 + i]) for i, p in enumerate(parts)]
-        for one in ins:
-            one.start()
-        for one, two in zip(ins, outs):
-            one.wait()
-            two.start()
-        for two in outs:
-            two.wait()
+                  flag, node, ws, wn, bnd, column, remap, hub_ids, edge_src, edge_dst, one_dst, one_src, col_of, summed, degree,
+                  out_buf, sem):
+    flag_in = pltpu.make_async_copy(flag_hbm, flag, sem.at[0])
+    flag_in.start()
+    parts = [pl.ds(i * 192, 192) for i in range(4)]
+    ins = [pltpu.make_async_copy(fast_hbm.at[p, :], out_buf.at[p, :], sem.at[1 + i]) for i, p in enumerate(parts)]
+    outs = [pltpu.make_async_copy(out_buf.at[p, :], out_hbm.at[p, :], sem.at[5 + i]) for i, p in enumerate(parts)]
+    for one in ins:
+        one.start()
+    flag_in.wait()
+    for one, two in zip(ins, outs):
+        one.wait()
+        two.start()
+    for two in outs:
+        two.wait()
 
     @pl.when(flag[0, 0] != 0)
     def _():
-        pairs = [(node_hbm, node), (ws_hbm, ws), (wn_hbm, wn), (bnd_hbm, bnd), (hubs_hbm, hubs), (remap_hbm, remap)]
+        grp = lax.axis_index("grp")
+        me = lax.axis_index("dev")
+        pairs = [(node_hbm, node), (ws_hbm, ws), (wn_hbm, wn), (bnd_hbm, bnd), (column_hbm, column), (remap_hbm, remap),
+                 (hub_hbm, hub_ids), (src_hbm, edge_src), (dst_hbm, edge_dst)]
         copies = [pltpu.make_async_copy(a, b, sem.at[i]) for i, (a, b) in enumerate(pairs)]
         for one in copies:
             one.start()
         for one in copies:
             one.wait()
+        owner, rank = hub_owner_rank(hub_ids[...])
+        at_row = place(owner % N_DEV, me) * COLUMN + ((grp - owner // N_DEV) & 7) * 2 + rank
+        choose = jnp.where(lax.broadcasted_iota(I32, (N_DEV * COLUMN, HUBS), 0) == at_row, 1.0, 0.0).astype(BF16)
+        hubs = dot(choose, column[...], TN).astype(BF16)
         col_of[...] = edge_column(edge_src[...], me)
         degree[...] = jnp.zeros_like(degree)
         summed[...] = jnp.zeros_like(summed)
@@ -357,7 +363,7 @@
         def _(g):
             block(HALO + g * 256, node[pl.ds(pl.multiple_of(g * 256, 256), 256), :])
 
-        block(HALO + NPD, hubs[...])
+        block(HALO + NPD, hubs)
         mean = (summed[...] / degree[...]).astype(BF16)
         mixed = dot(node[...], ws[...]) + dot(mean, wn[...])
         out_buf[...] = jnp.maximum(mixed, 0.0).astype(BF16)
@@ -377,18 +383,18 @@
         pltpu.VMEM((N_DEV * BND, D), BF16),
         pltpu.VMEM((N_DEV * 16, 128), BF16),
         pltpu.VMEM((N_DEV * COLUMN, D), BF16),
-        pltpu.VMEM((HUBS, D), BF16),
         pltpu.VMEM((N_GRP, 16, 128), BF16),
         pltpu.VMEM((N_DEV * BND, 256), BF16),
         pltpu.VMEM((ROWS, 128), I32),
         pltpu.VMEM((ROWS, 128), F32),
         pltpu.VMEM((NPD, STEP), BF16),
-        pltpu.VMEM((NPD, STEP), BF16),
-        pltpu.VMEM((LINES, STEP), BF16),
         pltpu.VMEM((LINES, STEP), BF16),
         pltpu.VMEM((LINES, NPD), F32),
+        pltpu.VMEM((NPD, 128), F32),
         pltpu.VMEM((HALO_DIGITS * HALO_LINES, NPD), BF16),
-        pltpu.VMEM((NPD + HUBS, NPD), BF16),
+        pltpu.VMEM((NPD, NPD), BF16),
+        pltpu.VMEM((HUBS, NPD), BF16),
+        pltpu.VMEM((N_DEV * COLUMN, NPD), BF16),
         pltpu.VMEM((N_DEV * BND, NPD), BF16),
         pltpu.VMEM((NPD, D), F32),
         pltpu.VMEM((NPD, D), F32),
@@ -398,11 +404,12 @@
     outs = [
         jax.ShapeDtypeStruct((NPD, D), BF16),
         jax.ShapeDtypeStruct((N_DEV * BND, D), BF16),
-        jax.ShapeDtypeStruct((HUBS, D), BF16),
+        jax.ShapeDtypeStruct((N_DEV * COLUMN, D), BF16),
         jax.ShapeDtypeStruct((N_DEV * BND, 256), BF16),
         jax.ShapeDtypeStruct((8, 128), I32),
     ]
-    fast, bnd, hubs, remap, flag = pl.pallas_call(
+    hub_row = hub_ids.reshape(1, HUBS)
+    fast, bnd, column, remap, flag = pl.pallas_call(
         main_kernel,
         out_shape=outs,
         in_specs=[any_, any_, any_, vmem, vmem, vmem, vmem, vmem],
@@ -412,31 +419,35 @@
             collective_id=0, has_side_effects=True, vmem_limit_bytes=56 * 2**20
         ),
         name="sage_main",
-    )(node_rows, w_self, w_neigh, hub_ids.reshape(1, HUBS), bnd_idx, send_pos, src, dst)
+    )(node_rows, w_self, w_neigh, hub_row, bnd_idx, send_pos, src, dst)
     scratch = [
+        pltpu.SMEM((8, 128), I32),
         pltpu.VMEM((NPD, D), BF16),
         pltpu.VMEM((D, D), BF16),
         pltpu.VMEM((D, D), BF16),
         pltpu.VMEM((N_DEV * BND, D), BF16),
-        pltpu.VMEM((HUBS, D), BF16),
+        pltpu.VMEM((N_DEV * COLUMN, D), BF16),
         pltpu.VMEM((N_DEV * BND, 256), BF16),
+        pltpu.VMEM((1, HUBS), I32),
+        pltpu.VMEM((ROWS, 128), I32),
+        pltpu.VMEM((ROWS, 128), I32),
         pltpu.VMEM((NPD, E_DEV), BF16),
         pltpu.VMEM((256, E_DEV), BF16),
         pltpu.VMEM((ROWS, 128), I32),
         pltpu.VMEM((NPD, D), F32),
         pltpu.VMEM((NPD, 1), F32),
         pltpu.VMEM((NPD, D), BF16),
-        dma((8,)),
+        dma((9,)),
     ]
     return pl.pallas_call(
         finish_kernel,
         out_shape=jax.ShapeDtypeStruct((NPD, D), BF16),
-        in_specs=[pl.BlockSpec(memory_space=pltpu.SMEM)] + [any_] * 7 + [vmem, vmem],
+        in_specs=[any_] * 11,
         out_specs=any_,
         scratch_shapes=scratch,
         compiler_params=pltpu.CompilerParams(vmem_limit_bytes=56 * 2**20),
         name="sage_finish",
-    )(flag, fast, node_rows, w_self, w_neigh, bnd, hubs, remap, src, dst)
+    )(flag, fast, node_rows, w_self, w_neigh, bnd, column, remap, hub_row, src, dst)
 
 
 def solution(mesh):

time: 43 us -> 40.1 us (0.933)
  Pallas kernels: 42.6 us -> 39.8 us
    pallas_call x1, Pallas kernels: 39.7 us -> 37.6 us  [body(): pl.pallas_call(main_kernel, out_shape=outs, in_specs=[any_, any_, any_, v...]
    pallas_call x1, Pallas kernels: 2.97 us -> 2.21 us  [body(): pl.pallas_call(finish_kernel, out_shape=jax.ShapeDtypeStruct((NPD, D), BF...]
where the time goes in v3:
time: 40.1 us; the launch traced here: 40 us
  Pallas kernels  39.8 us (99%)
    pallas_call x1, Pallas kernels, body(): pl.pallas_call(main_kernel, out_shape=outs, in_specs=[any_, any_, any_, v...  37.6 us
    pallas_call x1, Pallas kernels, body(): pl.pallas_call(finish_kernel, out_shape=jax.ShapeDtypeStruct((NPD, D), BF...  2.21 us

profile of v3, /device:TPU:1, one launch (start us, length us, event | category | flops | bytes accessed | tf_op | source)
XLA Modules:
  0.0 40.0 jit_solution(17555091268604677831)
XLA Ops:
  0.0 37.6 %sage_main.1 = (bf16[768,1024]{1,0:T(8,128)(2,1)}, bf16[1024,1024]{1,0:T(8,128)(2,1)}, bf16[512,1024]{1,0:T(8,128)(2,1)}, bf16[1024,256]{1,0:T(8,128)(2,1)}, s32[8,128]{1,0:T(8,128)}) custom-call(bf16[768,1024]{1,0:T(8,128)(2,1)} %node_hbm.3, bf16[1024,1024]{1,0:T(8,128)(2,1)} %ws_hbm.3, bf16[1024,1024]{1,0:T(8,128)(2,1)} %wn_hbm.3, s32[1,64]{1,0:T(1,128)} %bitcast.7, ...), custom_call_target="tpu_custom_call" | custom-call | tf_op jit(solution)/shard_map/sage_main/pallas_call | solution.py:412
  37.6 2.2 %sage_finish.1 = bf16[768,1024]{1,0:T(8,128)(2,1)} custom-call(s32[8,128]{1,0:T(8,128)} %get-tuple-element.10.flag_hbm, bf16[768,1024]{1,0:T(8,128)(2,1)} %get-tuple-element.11.fast_hbm, bf16[768,1024]{1,0:T(8,128)(2,1)} %node_hbm.3, bf16[1024,1024]{1,0:T(8,128)(2,1)} %ws_hbm.3, bf16[1024,1024]{1,0:T(8,128)(2,1)} %wn_hbm.3, ...), custom_call_target="tpu_custom_call" | custom-call | tf_op jit(solution)/shard_map/sage_finish/pallas_call | solution.py:442

commit v4 on v3

--- a/solution.py
+++ b/solution.py
@@ -127,6 +127,13 @@
     tile = jnp.concatenate([pair[0:2, q * 128 : (q + 1) * 128] for q in range(8)], axis=0)
     tile_z[0] = tile.astype(BF16)
 
+    pl.semaphore_wait(barrier, 7 + N_GRP - 1)
+    for o in range(1, N_GRP):
+        copy(tile_z.at[0], tile_z.at[o], z_send, 2, (grp + o) % N_GRP, me)
+    spread_u(pos, 16, p_send, 1)
+    spread_u(bnd, BND, b_send, 0)
+    spread_sib(bnd, BND, 0, 1, b_sib_send, 3)
+
     col = edge_column(edge_src[...], me)
     third = lambda n: (n * 43) >> 7
     own = col - HALO
@@ -138,20 +145,8 @@
     line_of[...] = line
     weight_of[...] = jnp.left_shift(jnp.ones_like(shift), shift).astype(F32)
 
-    distance = jnp.minimum(grp, N_GRP - grp)
-    first_send = jnp.maximum(2 - distance, 0)
-
     @pl.loop(0, STEPS)
     def _(step):
-        @pl.when(step == first_send)
-        def _():
-            pl.semaphore_wait(barrier, 7 + N_GRP - 1)
-            for o in range(1, N_GRP):
-                copy(tile_z.at[0], tile_z.at[o], z_send, 2, (grp + o) % N_GRP, me)
-            spread_u(bnd, BND, b_send, 0)
-            spread_u(pos, 16, p_send, 1)
-            spread_sib(bnd, BND, 0, 1, b_sib_send, 3)
-
         zero, one = jnp.zeros((), BF16), jnp.ones((), BF16)
         for r in range(STEP_ROWS):
             row = pl.ds(step * STEP_ROWS + r, 1)
@@ -165,118 +160,149 @@
             one_src[:, here] = jnp.where(lines >= DEGREE_AT, one, value)
         packed[...] += dot(one_src[...], one_dst[...], NT)
 
-        @pl.when(step == first_send)
+        @pl.when(step == 0)
         def _():
             spread_v(bnd, BND, 0, 1, b_send, 4)
 
-    total = jnp.zeros((1, NPD), I32)
-    ints = packed[0:HALO_LINES, :].astype(I32)
-    for i in range(HALO_DIGITS):
-        digit = ints >> (HALO_BITS * i)
-        if i < HALO_DIGITS - 1:
-            digit = digit & (2**HALO_BITS - 1)
-        total = total + jnp.sum(digit, axis=0, keepdims=True)
-        halo_cnt[i * HALO_LINES : (i + 1) * HALO_LINES, :] = digit.astype(F32).astype(BF16)
-    ints = packed[HALO_LINES:DEGREE_AT, :].astype(I32)
-    hub_parts = []
-    for i in range(OWN_DIGITS):
-        digit = ints >> (OWN_BITS * i)
-        if i < OWN_DIGITS - 1:
-            digit = digit & (2**OWN_BITS - 1)
-        total = total + jnp.sum(digit, axis=0, keepdims=True)
-        digit = digit.astype(F32)
-        own_cnt[i * OWN_LINES : (i + 1) * OWN_LINES, :] = digit[0:OWN_LINES].astype(BF16)
-        hub_parts.append(digit[OWN_LINES:])
-    hub_cnt[...] = jnp.concatenate(hub_parts, axis=0).astype(BF16)
-
-    degree = packed[DEGREE_AT : DEGREE_AT + 1, :]
-    largest = jnp.max(packed[0:DEGREE_AT, :], axis=0, keepdims=True)
-    bad = (total != degree.astype(I32)) | (largest >= LIMIT) | (degree > 256.0)
-    flag[...] = jnp.broadcast_to(jnp.max(jnp.where(bad, 1, 0), axis=1, keepdims=True), (8, 128))
-    inverse[...] = jnp.transpose(jnp.broadcast_to(1.0 / degree, (128, NPD)))
+        @pl.when(step == 3)
+        def _():
+            done(pos, 16, 3, recv.at[1])
+            spread_v(pos, 16, 0, 4, p_send, 6)
+            done(bnd, BND, 3, recv.at[0])
+            spread_v(bnd, BND, 1, 3, b_send, 5)
+            spread_sib(bnd, BND, 1, 3, b_sib_send, 3)
+
+            part = tile_z.at[pl.ds(1, N_GRP - 1)]
+            pltpu.make_async_copy(part, part, recv.at[2]).wait()
+            tiles = [tile_z[o].astype(F32) for o in range(N_GRP)]
+            for q in range(8):
+                rows = jnp.concatenate([t[2 * q : 2 * q + 2, :] for t in tiles], axis=0)
+                column[0:COLUMN, q * 128 : (q + 1) * 128] = rows.astype(BF16)
+            spread_u(column, COLUMN, h_send, 7)
+
+    bnd_out = pltpu.make_async_copy(bnd, bnd_hbm, out_sem.at[0])
+    column_out = pltpu.make_async_copy(column, column_hbm, out_sem.at[1])
+    remap_out = pltpu.make_async_copy(remap, remap_hbm, out_sem.at[2])
 
     def third_of(i):
         return slice(i * 256, (i + 1) * 256)
 
-    done(bnd, BND, 3, recv.at[0])
-    spread_v(bnd, BND, 1, 3, b_send, 5)
-    done(pos, 16, 3, recv.at[1])
-    spread_v(pos, 16, 0, 4, p_send, 6)
-    spread_sib(bnd, BND, 1, 3, b_sib_send, 3)
-
-    ws_in.wait()
-    for i in range(3):
-        acc[third_of(i), :] = dot(node[third_of(i), :], ws[...])
-
-    for i in range(3):
-        summed[third_of(i), :] = dot(own_cnt[0:NPD, third_of(i)], node[...], TN)
-
-    part = tile_z.at[pl.ds(1, N_GRP - 1)]
-    pltpu.make_async_copy(part, part, recv.at[2]).wait()
-    tiles = [tile_z[o].astype(F32) for o in range(N_GRP)]
-    for q in range(8):
-        rows = jnp.concatenate([t[2 * q : 2 * q + 2, :] for t in tiles], axis=0)
-        column[0:COLUMN, q * 128 : (q + 1) * 128] = rows.astype(BF16)
-    spread_u(column, COLUMN, h_send, 7)
-
-    done(pos, 16, 12, recv.at[6])
-    spread_sib(pos, 16, 0, 16, p_sib_send, 10)
-
-    at_row = place(owner % N_DEV, me) * COLUMN + ((grp - owner // N_DEV) & 7) * 2 + rank
-    choose = jnp.where(lax.broadcasted_iota(I32, (N_DEV * COLUMN, HUBS), 0) == at_row, 1.0, 0.0).astype(BF16)
-    column_cnt[...] = dot(choose, hub_cnt[...]).astype(BF16)
-
-    done(column, COLUMN, 3, recv.at[7])
-    spread_v(column, COLUMN, 0, 4, h_send, 8)
-    spread_sib(column, COLUMN, 0, 4, h_sib_send, 9)
-
-    done(pos, 16, 16, recv.at[10])
-    every = pos[...].astype(F32).reshape(N_DEV, 16, 128)
-    mine = lax.broadcasted_iota(I32, (N_DEV, 16, 128), 1) == me % 16
-    rows = jnp.sum(jnp.where(mine, every, 0.0), axis=1)
-    turned = pltpu.roll(rows, SLOT, 1)
-    low = jnp.where(me < 16, rows, turned)
-    high = jnp.where(me < 16, turned, rows)
-    lane = lax.broadcasted_iota(I32, (128, 128), 1)
-    line = lax.broadcasted_iota(I32, (128, 128), 0)
-    for g in range(8):
-        for half in range(2):
-            a = 4 * g + 2 * half
-            wanted = jnp.where(lane < SLOT, low[a : a + 1, :], high[a + 1 : a + 2, :]).astype(I32)
-            match = ((line >> 5) == 2 * half + (lane >> 6)) & ((line & 31) == wanted)
-            remap[g * 128 : (g + 1) * 128, half * 128 : (half + 1) * 128] = jnp.where(match, 1.0, 0.0).astype(BF16)
-    for g in range(8):
-        part = dot(remap[g * 128 : (g + 1) * 128, :], halo_cnt[g * 256 : (g + 1) * 256, :])
-        bnd_cnt[g * 128 : (g + 1) * 128, :] = part.astype(BF16)
-    remap_out = pltpu.make_async_copy(remap, remap_hbm, out_sem.at[2])
-    remap_out.start()
-
-    done(bnd, BND, 3, recv.at[4])
-    done(bnd, BND, 9, recv.at[5])
-    spread_sib(bnd, BND, 4, 12, b_sib_send, 11)
-    for i in range(3):
-        summed[third_of(i), :] += dot(bnd_cnt[0:512, third_of(i)], bnd[0:512, :], TN)
-
-    done(column, COLUMN, 12, recv.at[8])
-    spread_sib(column, COLUMN, 4, 12, h_sib_send, 9)
-
-    done(bnd, BND, 4, recv.at[3])
-    done(bnd, BND, 12, recv.at[11])
-    bnd_out = pltpu.make_async_copy(bnd, bnd_hbm, out_sem.at[0])
-    bnd_out.start()
-    for i in range(3):
-        summed[third_of(i), :] += dot(bnd_cnt[512:, third_of(i)], bnd[512:, :], TN)
-
-    wn_in.wait()
-    done(column, COLUMN, 16, recv.at[9])
-    column_out = pltpu.make_async_copy(column, column_hbm, out_sem.at[1])
-    column_out.start()
-    for i in range(3):
-        total = summed[third_of(i), :] + dot(column_cnt[:, third_of(i)], column[...], TN)
-        mean = (total * jnp.concatenate([inverse[third_of(i), :]] * 8, axis=1)).astype(BF16)
-        mixed = acc[third_of(i), :] + dot(mean, wn[...])
-        out_buf[third_of(i), :] = jnp.maximum(mixed, 0.0).astype(BF16)
-        pltpu.make_async_copy(out_buf.at[third_of(i), :], out_hbm.at[third_of(i), :], out_sem.at[3]).start()
+    def task(run):
+        pl.when(me >= 0)(run)
+
+    @task
+    def _():
+        total = jnp.zeros((1, NPD), I32)
+        ints = packed[0:HALO_LINES, :].astype(I32)
+        for i in range(HALO_DIGITS):
+            digit = ints >> (HALO_BITS * i)
+            if i < HALO_DIGITS - 1:
+                digit = digit & (2**HALO_BITS - 1)
+            total = total + jnp.sum(digit, axis=0, keepdims=True)
+            halo_cnt[i * HALO_LINES : (i + 1) * HALO_LINES, :] = digit.astype(F32).astype(BF16)
+        ints = packed[HALO_LINES:DEGREE_AT, :].astype(I32)
+        hub_parts = []
+        for i in range(OWN_DIGITS):
+            digit = ints >> (OWN_BITS * i)
+            if i < OWN_DIGITS - 1:
+                digit = digit & (2**OWN_BITS - 1)
+            total = total + jnp.sum(digit, axis=0, keepdims=True)
+            digit = digit.astype(F32)
+            own_cnt[i * OWN_LINES : (i + 1) * OWN_LINES, :] = digit[0:OWN_LINES].astype(BF16)
+            hub_parts.append(digit[OWN_LINES:])
+        hub_cnt[...] = jnp.concatenate(hub_parts, axis=0).astype(BF16)
+
+        degree = packed[DEGREE_AT : DEGREE_AT + 1, :]
+        largest = jnp.max(packed[0:DEGREE_AT, :], axis=0, keepdims=True)
+        bad = (total != degree.astype(I32)) | (largest >= LIMIT) | (degree > 256.0)
+        flag[...] = jnp.broadcast_to(jnp.max(jnp.where(bad, 1, 0), axis=1, keepdims=True), (8, 128))
+        inverse[...] = jnp.transpose(jnp.broadcast_to(1.0 / degree, (128, NPD)))
+
+    @task
+    def _():
+        ws_in.wait()
+        for i in range(3):
+            acc[third_of(i), :] = dot(node[third_of(i), :], ws[...])
+
+    @task
+    def _():
+        done(column, COLUMN, 3, recv.at[7])
+        spread_v(column, COLUMN, 0, 4, h_send, 8)
+        spread_sib(column, COLUMN, 0, 4, h_sib_send, 9)
+
+    @task
+    def _():
+        for i in range(3):
+            summed[third_of(i), :] = dot(own_cnt[0:NPD, third_of(i)], node[...], TN)
+
+    @task
+    def _():
+        at_row = place(owner % N_DEV, me) * COLUMN + ((grp - owner // N_DEV) & 7) * 2 + rank
+        choose = jnp.where(lax.broadcasted_iota(I32, (N_DEV * COLUMN, HUBS), 0) == at_row, 1.0, 0.0).astype(BF16)
+        column_cnt[...] = dot(choose, hub_cnt[...]).astype(BF16)
+
+    @task
+    def _():
+        done(pos, 16, 12, recv.at[6])
+        spread_sib(pos, 16, 0, 16, p_sib_send, 10)
+
+    @task
+    def _():
+        done(pos, 16, 16, recv.at[10])
+        every = pos[...].astype(F32).reshape(N_DEV, 16, 128)
+        mine = lax.broadcasted_iota(I32, (N_DEV, 16, 128), 1) == me % 16
+        rows = jnp.sum(jnp.where(mine, every, 0.0), axis=1)
+        turned = pltpu.roll(rows, SLOT, 1)
+        low = jnp.where(me < 16, rows, turned)
+        high = jnp.where(me < 16, turned, rows)
+        lane = lax.broadcasted_iota(I32, (128, 128), 1)
+        line = lax.broadcasted_iota(I32, (128, 128), 0)
+        for g in range(8):
+            for half in range(2):
+                a = 4 * g + 2 * half
+                wanted = jnp.where(lane < SLOT, low[a : a + 1, :], high[a + 1 : a + 2, :]).astype(I32)
+                match = ((line >> 5) == 2 * half + (lane >> 6)) & ((line & 31) == wanted)
+                remap[g * 128 : (g + 1) * 128, half * 128 : (half + 1) * 128] = jnp.where(match, 1.0, 0.0).astype(BF16)
+        for g in range(8):
+            part = dot(remap[g * 128 : (g + 1) * 128, :], halo_cnt[g * 256 : (g + 1) * 256, :])
+            bnd_cnt[g * 128 : (g + 1) * 128, :] = part.astype(BF16)
+        remap_out.start()
+
+    @task
+    def _():
+        done(bnd, BND, 3, recv.at[4])
+        done(bnd, BND, 9, recv.at[5])
+        spread_sib(bnd, BND, 4, 12, b_sib_send, 11)
+
+    @task
+    def _():
+        for i in range(3):
+            summed[third_of(i), :] += dot(bnd_cnt[0:512, third_of(i)], bnd[0:512, :], TN)
+
+    @task
+    def _():
+        done(column, COLUMN, 12, recv.at[8])
+        spread_sib(column, COLUMN, 4, 12, h_sib_send, 9)
+
+    @task
+    def _():
+        done(bnd, BND, 4, recv.at[3])
+        done(bnd, BND, 12, recv.at[11])
+        bnd_out.start()
+        for i in range(3):
+            summed[third_of(i), :] += dot(bnd_cnt[512:, third_of(i)], bnd[512:, :], TN)
+
+    @task
+    def _():
+        wn_in.wait()
+        done(column, COLUMN, 16, recv.at[9])
+        column_out.start()
+        for i in range(3):
+            total = summed[third_of(i), :] + dot(column_cnt[:, third_of(i)], column[...], TN)
+            mean = (total * jnp.concatenate([inverse[third_of(i), :]] * 8, axis=1)).astype(BF16)
+            mixed = acc[third_of(i), :] + dot(mean, wn[...])
+            out_buf[third_of(i), :] = jnp.maximum(mixed, 0.0).astype(BF16)
+            pltpu.make_async_copy(out_buf.at[third_of(i), :], out_hbm.at[third_of(i), :], out_sem.at[3]).start()
 
     done(bnd, BND, 15, b_send)
     done(bnd, BND, 16, b_sib_send)

time: 40.1 us -> 36.8 us (0.918)
  Pallas kernels: 39.8 us -> 36.4 us
    pallas_call x1, Pallas kernels: 37.6 us -> 34.2 us  [body(): pl.pallas_call(main_kernel, out_shape=outs, in_specs=[any_, any_, any_, v...]
where the time goes in v4:
time: 36.8 us; the launch traced here: 36.6 us
  Pallas kernels  36.4 us (99%)
    pallas_call x1, Pallas kernels, body(): pl.pallas_call(main_kernel, out_shape=outs, in_specs=[any_, any_, any_, v...  34.2 us
    pallas_call x1, Pallas kernels, body(): pl.pallas_call(finish_kernel, out_shape=jax.ShapeDtypeStruct((NPD, D), BF...  2.21 us

profile of v4, /device:TPU:1, one launch (start us, length us, event | category | flops | bytes accessed | tf_op | source)
XLA Modules:
  0.0 36.6 jit_solution(4436377418825889043)
XLA Ops:
  0.0 34.2 %sage_main.1 = (bf16[768,1024]{1,0:T(8,128)(2,1)}, bf16[1024,1024]{1,0:T(8,128)(2,1)}, bf16[512,1024]{1,0:T(8,128)(2,1)}, bf16[1024,256]{1,0:T(8,128)(2,1)}, s32[8,128]{1,0:T(8,128)}) custom-call(bf16[768,1024]{1,0:T(8,128)(2,1)} %node_hbm.3, bf16[1024,1024]{1,0:T(8,128)(2,1)} %ws_hbm.3, bf16[1024,1024]{1,0:T(8,128)(2,1)} %wn_hbm.3, s32[1,64]{1,0:T(1,128)} %bitcast.7, ...), custom_call_target="tpu_custom_call" | custom-call | tf_op jit(solution)/shard_map/sage_main/pallas_call | solution.py:438
  34.2 2.2 %sage_finish.1 = bf16[768,1024]{1,0:T(8,128)(2,1)} custom-call(s32[8,128]{1,0:T(8,128)} %get-tuple-element.10.flag_hbm, bf16[768,1024]{1,0:T(8,128)(2,1)} %get-tuple-element.11.fast_hbm, bf16[768,1024]{1,0:T(8,128)(2,1)} %node_hbm.3, bf16[1024,1024]{1,0:T(8,128)(2,1)} %ws_hbm.3, bf16[1024,1024]{1,0:T(8,128)(2,1)} %wn_hbm.3, ...), custom_call_target="tpu_custom_call" | custom-call | tf_op jit(solution)/shard_map/sage_finish/pallas_call | solution.py:468

commit v5 on v4

--- a/solution.py
+++ b/solution.py
@@ -84,10 +84,10 @@
     wn_in.start()
 
     barrier = pltpu.get_barrier_semaphore()
+    for o in (4, 5, 3, 6, 2, 7, 1):
+        pl.semaphore_signal(barrier, inc=1, device_id=((grp + o) % N_GRP, me), device_id_type=MESH)
     for near in [at(1, 0), at(3, 0), at(2, 0), at(0, 1), at(0, 3), at(0, 2), sib]:
         pl.semaphore_signal(barrier, inc=1, device_id=(grp, near), device_id_type=MESH)
-    for o in range(1, N_GRP):
-        pl.semaphore_signal(barrier, inc=1, device_id=((grp + o) % N_GRP, me), device_id_type=MESH)
 
     packed[...] = jnp.zeros_like(packed)
 
@@ -128,7 +128,7 @@
     tile_z[0] = tile.astype(BF16)
 
     pl.semaphore_wait(barrier, 7 + N_GRP - 1)
-    for o in range(1, N_GRP):
+    for o in (4, 5, 3, 6, 2, 7, 1):
         copy(tile_z.at[0], tile_z.at[o], z_send, 2, (grp + o) % N_GRP, me)
     spread_u(pos, 16, p_send, 1)
     spread_u(bnd, BND, b_send, 0)
@@ -166,12 +166,6 @@
 
         @pl.when(step == 3)
         def _():
-            done(pos, 16, 3, recv.at[1])
-            spread_v(pos, 16, 0, 4, p_send, 6)
-            done(bnd, BND, 3, recv.at[0])
-            spread_v(bnd, BND, 1, 3, b_send, 5)
-            spread_sib(bnd, BND, 1, 3, b_sib_send, 3)
-
             part = tile_z.at[pl.ds(1, N_GRP - 1)]
             pltpu.make_async_copy(part, part, recv.at[2]).wait()
             tiles = [tile_z[o].astype(F32) for o in range(N_GRP)]
@@ -179,6 +173,12 @@
                 rows = jnp.concatenate([t[2 * q : 2 * q + 2, :] for t in tiles], axis=0)
                 column[0:COLUMN, q * 128 : (q + 1) * 128] = rows.astype(BF16)
             spread_u(column, COLUMN, h_send, 7)
+
+            done(pos, 16, 3, recv.at[1])
+            spread_v(pos, 16, 0, 4, p_send, 6)
+            done(bnd, BND, 3, recv.at[0])
+            spread_v(bnd, BND, 1, 3, b_send, 5)
+            spread_sib(bnd, BND, 1, 3, b_sib_send, 3)
 
     bnd_out = pltpu.make_async_copy(bnd, bnd_hbm, out_sem.at[0])
     column_out = pltpu.make_async_copy(column, column_hbm, out_sem.at[1])
@@ -283,6 +283,8 @@
     def _():
         done(column, COLUMN, 12, recv.at[8])
         spread_sib(column, COLUMN, 4, 12, h_sib_send, 9)
+        for i in range(3):
+            summed[third_of(i), :] += dot(column_cnt[0:256, third_of(i)], column[0:256, :], TN)
 
     @task
     def _():
@@ -298,7 +300,7 @@
         done(column, COLUMN, 16, recv.at[9])
         column_out.start()
         for i in range(3):
-            total = summed[third_of(i), :] + dot(column_cnt[:, third_of(i)], column[...], TN)
+            total = summed[third_of(i), :] + dot(column_cnt[256:, third_of(i)], column[256:, :], TN)
             mean = (total * jnp.concatenate([inverse[third_of(i), :]] * 8, axis=1)).astype(BF16)
             mixed = acc[third_of(i), :] + dot(mean, wn[...])
             out_buf[third_of(i), :] = jnp.maximum(mixed, 0.0).astype(BF16)

time: 36.8 us -> 36.5 us (level)
  no operation moved by 1% of the time
where the time goes in v5:
time: 36.5 us; the launch traced here: 36.3 us
  Pallas kernels  36.1 us (99%)
    pallas_call x1, Pallas kernels, body(): pl.pallas_call(main_kernel, out_shape=outs, in_specs=[any_, any_, any_, v...  33.9 us
    pallas_call x1, Pallas kernels, body(): pl.pallas_call(finish_kernel, out_shape=jax.ShapeDtypeStruct((NPD, D), BF...  2.21 us

profile of v5, /device:TPU:1, one launch (start us, length us, event | category | flops | bytes accessed | tf_op | source)
XLA Modules:
  0.0 36.3 jit_solution(6824547666219045081)
XLA Ops:
  0.0 33.9 %sage_main.1 = (bf16[768,1024]{1,0:T(8,128)(2,1)}, bf16[1024,1024]{1,0:T(8,128)(2,1)}, bf16[512,1024]{1,0:T(8,128)(2,1)}, bf16[1024,256]{1,0:T(8,128)(2,1)}, s32[8,128]{1,0:T(8,128)}) custom-call(bf16[768,1024]{1,0:T(8,128)(2,1)} %node_hbm.3, bf16[1024,1024]{1,0:T(8,128)(2,1)} %ws_hbm.3, bf16[1024,1024]{1,0:T(8,128)(2,1)} %wn_hbm.3, s32[1,64]{1,0:T(1,128)} %bitcast.7, ...), custom_call_target="tpu_custom_call" | custom-call | tf_op jit(solution)/shard_map/sage_main/pallas_call | solution.py:440
  33.9 2.2 %sage_finish.1 = bf16[768,1024]{1,0:T(8,128)(2,1)} custom-call(s32[8,128]{1,0:T(8,128)} %get-tuple-element.10.flag_hbm, bf16[768,1024]{1,0:T(8,128)(2,1)} %get-tuple-element.11.fast_hbm, bf16[768,1024]{1,0:T(8,128)(2,1)} %node_hbm.3, bf16[1024,1024]{1,0:T(8,128)(2,1)} %ws_hbm.3, bf16[1024,1024]{1,0:T(8,128)(2,1)} %wn_hbm.3, ...), custom_call_target="tpu_custom_call" | custom-call | tf_op jit(solution)/shard_map/sage_finish/pallas_call | solution.py:470
